TPU v7x, 256 devices: a whole 4x4x8 slice. The times are simulated.
256 devices in a mesh: section: 8 (over x_lo, y), ctx: 32 (over z, x_hi, core).
Axes of the slice: x: 4 (x_hi: 2, x_lo: 2; x = x_hi * 2 + x_lo), y: 4, z: 8, core: 2. Of those that a mesh axis runs over, the one named last changes fastest.
Arguments:
- embeds: bfloat16 [4096, 2048], P('ctx'), may hold values from -7 to 7
- q_weight: bfloat16 [8, 2048, 1024], P('section'), may hold values from -1 to 1
- out_weight: bfloat16 [8, 1024, 2048], P('section'), may hold values from -0.1875 to 0.1875
- norm_gain: bfloat16 [8, 2048], P('section'), may hold values from 0.3984375 to 2.5
- kv_weight: bfloat16 [2048, 512], replicated, may hold values from -1 to 1
- kv_gain: bfloat16 [2048], replicated, may hold values from 0.5 to 1.5
- block_slot: int32 [32], replicated, may hold values from 0 to 31, each once
Outputs:
- layer_out: bfloat16 [8, 4096, 2048], P('section', 'ctx')
- decode_cache: bfloat16 [32, 128, 512], P('ctx', None, 'section')
Inputs may be any that keep to these rules, and one draw needn't show every extreme that they name: `block_slot`: every slot is named by exactly one block; slot s is kept by ctx index s // 1.
All inputs are finite; a program needn't handle non-finite values.
Results may differ from a plain program's by a relative error of at most 0.025.
Values may be sent and summed in bfloat16 or wider, within the bound.
A program may use at most 128 MiB of HBM per device.

v0:
```python
import math

import jax
import jax.numpy as jnp
from jax import lax
from jax.sharding import PartitionSpec as P

QUERY_HEADS = 16
KEY_VALUE_HEADS = 4
HEAD_SIZE = 64
BLOCK = 128
ITERS = 3


EPS = 1e-05


def broadcast(value, axis, source):
    kept = jnp.where(lax.axis_index(axis) == source, value, 0).astype(value.dtype)
    return lax.psum(kept, axis)


def from_behind(value, axis, steps):
    count = lax.axis_size(axis)
    first, last = (max(0, -steps), min(count, count - steps))
    return lax.ppermute(value, axis, [(source, source + steps) for source in range(first, last)])


def normalize(value_rows, gain):
    wide = value_rows.astype(jnp.float32)
    factor = lax.rsqrt(jnp.mean(wide * wide, axis=-1, keepdims=True) + EPS)
    return wide * factor * gain.astype(jnp.float32)


def project_cache(hidden, kv_gain, kv_weight):
    normed = normalize(hidden, kv_gain).astype(jnp.bfloat16)
    return jnp.dot(normed, kv_weight, preferred_element_type=jnp.float32).astype(jnp.bfloat16)


def online_update(loop_state, query_rows, qpos, key_rows, value_rows, kpos):
    maxima, totals, accum = loop_state
    scores = jnp.einsum(
        "igrd,jgd->grij", query_rows, key_rows, preferred_element_type=jnp.float32
    ) * HEAD_SIZE ** (-0.5)
    allowed = kpos[None, :] <= qpos[:, None]
    scores = jnp.where(allowed, scores, -1e30)
    newmax = jnp.maximum(maxima, jnp.max(scores, axis=-1))
    probs = jnp.where(allowed, jnp.exp(scores - newmax[..., None]), 0.0)
    decay = jnp.exp(maxima - newmax)
    update = jnp.einsum(
        "grij,jgd->grid", probs.astype(jnp.bfloat16), value_rows, preferred_element_type=jnp.float32
    )
    return (newmax, decay * totals + jnp.sum(probs, axis=-1), decay[..., None] * accum + update)


def attend_piece(loop_state, query_rows, qpos, piece):
    length = piece.shape[0]
    feature_width = math.gcd(length, 512)
    number = length // feature_width
    half_width = KEY_VALUE_HEADS * HEAD_SIZE
    blocks = piece.reshape(number, feature_width, piece.shape[1])

    def one_block(state, inputs):
        block_rows, index = inputs
        key_offset = index * feature_width

        def update(inner):
            key_rows = block_rows[:, :half_width].reshape(feature_width, KEY_VALUE_HEADS, HEAD_SIZE)
            value_rows = block_rows[:, half_width:].reshape(
                feature_width, KEY_VALUE_HEADS, HEAD_SIZE
            )
            kpos = key_offset + jnp.arange(feature_width, dtype=jnp.int32)
            return online_update(inner, query_rows, qpos, key_rows, value_rows, kpos)

        return (update(state), None)

    state, _ = lax.scan(one_block, loop_state, (blocks, jnp.arange(number, dtype=jnp.int32)))
    return state


def body(embeds, q_weight, out_weight, norm_gain, kv_weight, kv_gain, block_slot):
    row_count = embeds.shape[0]
    sections = lax.axis_size("section")
    top = sections - 1
    section_index = lax.axis_index("section")
    ctx_index = lax.axis_index("ctx")
    query_groups = QUERY_HEADS // KEY_VALUE_HEADS
    qpos = ctx_index * row_count + jnp.arange(row_count, dtype=jnp.int32)
    cache_local = project_cache(embeds, kv_gain, kv_weight)
    hidden_in = embeds
    hidden_out = embeds
    for step in range(ITERS):
        normed = normalize(hidden_in, norm_gain[0]).astype(jnp.bfloat16)
        query_rows = jnp.dot(normed, q_weight[0], preferred_element_type=jnp.float32).astype(
            jnp.bfloat16
        )
        query_rows = query_rows.reshape(row_count, KEY_VALUE_HEADS, query_groups, HEAD_SIZE)
        start_state = (
            jnp.full((KEY_VALUE_HEADS, query_groups, row_count), -1e30, jnp.float32),
            jnp.zeros((KEY_VALUE_HEADS, query_groups, row_count), jnp.float32),
            jnp.zeros((KEY_VALUE_HEADS, query_groups, row_count, HEAD_SIZE), jnp.float32),
        )
        if step > 0:
            cache_local = broadcast(cache_local, "section", top)
        state = attend_piece(
            start_state, query_rows, qpos, lax.all_gather(cache_local, "ctx", axis=0, tiled=True)
        )
        merged = state[2] / state[1][..., None]
        mixed = (
            merged.transpose(2, 0, 1, 3)
            .reshape(row_count, QUERY_HEADS * HEAD_SIZE)
            .astype(jnp.bfloat16)
        )
        hidden_out = (
            hidden_in.astype(jnp.float32)
            + jnp.dot(mixed, out_weight[0], preferred_element_type=jnp.float32)
        ).astype(jnp.bfloat16)
        cache_local = project_cache(hidden_out, kv_gain, kv_weight)
        if step + 1 < ITERS:
            moved = from_behind(hidden_out, "section", 1)
            hidden_in = jnp.where(section_index == 0, embeds, moved)
    final = broadcast(cache_local, "section", top)
    feature_width = final.shape[1] // sections
    mine = lax.dynamic_slice_in_dim(final, section_index * feature_width, feature_width, 1)
    per_device = row_count // BLOCK
    owned = ctx_index * per_device + jnp.arange(per_device, dtype=jnp.int32)
    piece = lax.all_gather(mine, "ctx", axis=0, tiled=True)
    count = piece.shape[0] // BLOCK
    pick = (block_slot[None, :] == owned[:, None]).astype(jnp.bfloat16)
    placed = jnp.einsum(
        "qb,btc->qtc",
        pick,
        piece.reshape(count, BLOCK, feature_width),
        preferred_element_type=jnp.float32,
    )
    return (hidden_out[None], placed.astype(jnp.bfloat16))


def solution(mesh):
    placed = (
        P("ctx", None),
        P("section", None, None),
        P("section", None, None),
        P("section", None),
        P(),
        P(),
        P(),
    )
    return jax.shard_map(
        body,
        mesh=mesh,
        in_specs=placed,
        out_specs=(P("section", "ctx", None), P("ctx", None, "section")),
        check_vma=False,
    )
```

profile of v0, /device:TPU:1, one launch (start us, length us, event | category | flops | bytes accessed | tf_op | source)
XLA Modules:
  0.0 840.6 jit_solution(558271462752397714)
XLA Ops:
  12.3 3.1 fusion.77
  15.6 87.1 %all-gather.4.cloned.1.call-done = bf16[4096,512]{1,0:T(8,128)(2,1)} async-done(((bf16[128,512]{1,0:T(8,128)(2,1)}), bf16[4096,512]{1,0:T(8,128)(2,1)}) %all-gather.4.cloned.1.call-update) | async-done | bytes 4194320 | tf_op jit(solution)/shard_map/all_gather | solution.py:106
  102.7 87.2 %while.45 = (s32[]{:T(128)}, f32[4,4,128]{2,1,0:T(4,128)S(1)}, f32[4,4,128]{2,1,0:T(4,128)S(1)}, f32[4,4,128,64]{2,3,1,0:T(8,128)}, s32[8]{0:T(128)S(1)}, /*inde...) while((s32[]{:T(128)}, f32[4,4,128]{2,1,0:T(4,128)S(1)}, ...), condition=%wide.region_4.5_spmd.clone, body=%wide.region_1.4_spmd.clone.sunk | while | flops 282536576 | bytes 38933744 | solution.py:77
  105.4 2.7 fusion.179
  108.2 3.3 fusion.180
  116.3 2.7 fusion.179
  119.1 3.3 fusion.180
  127.2 2.7 fusion.179
  130.0 3.3 fusion.180
  138.1 2.7 fusion.179
  140.9 3.3 fusion.180
  149.0 2.7 fusion.179
  151.8 3.3 fusion.180
  160.0 2.7 fusion.179
  162.7 3.3 fusion.180
  170.9 2.7 fusion.179
  173.6 3.3 fusion.180
  181.8 2.7 fusion.179
  184.5 3.3 fusion.180
  191.0 3.2 fusion.91
  196.3 70.0 %all-reduce.4.cloned.1.call-done = bf16[128,512]{1,0:T(8,128)(2,1)} async-done(((bf16[128,512]{1,0:T(8,128)(2,1)}), bf16[128,512]{1,0:T(8,128)(2,1)}) %all-reduce.4.cloned.1.call-update) | async-done | bytes 131088 | tf_op jit(solution)/shard_map/psum | solution.py:20
  267.7 6.4 collective-permute-done
  275.2 3.0 fusion.80
  278.3 82.9 %all-gather.6.cloned.1.call-done = bf16[4096,512]{1,0:T(8,128)(2,1)} async-done(((bf16[128,512]{1,0:T(8,128)(2,1)}), bf16[4096,512]{1,0:T(8,128)(2,1)}) %all-gather.6.cloned.1.call-update) | async-done | bytes 4194320 | tf_op jit(solution)/shard_map/all_gather | solution.py:106
  361.2 87.2 %while.46 = (s32[]{:T(128)}, f32[4,4,128]{2,1,0:T(4,128)S(1)}, f32[4,4,128]{2,1,0:T(4,128)S(1)}, f32[4,4,128,64]{2,3,1,0:T(8,128)}, s32[8]{0:T(128)S(1)}, /*inde...) while((s32[]{:T(128)}, f32[4,4,128]{2,1,0:T(4,128)S(1)}, ...), condition=%wide.region_11.12_spmd.clone, body=%wide.region_8.11_spmd.clone.sunk | while | flops 282536576 | bytes 38933744 | solution.py:77
  364.0 2.7 fusion.188
  366.8 3.3 fusion.189
  374.9 2.7 fusion.188
  377.7 3.3 fusion.189
  385.8 2.7 fusion.188
  388.6 3.3 fusion.189
  396.7 2.7 fusion.188
  399.5 3.3 fusion.189
  410.4 3.3 fusion.189
  418.5 2.7 fusion.188
  421.3 3.3 fusion.189
  429.4 2.7 fusion.188
  432.2 3.3 fusion.189
  443.1 3.3 fusion.189
  449.6 3.2 fusion.94
  454.9 69.9 %all-reduce.6.cloned.1.call-done = bf16[128,512]{1,0:T(8,128)(2,1)} async-done(((bf16[128,512]{1,0:T(8,128)(2,1)}), bf16[128,512]{1,0:T(8,128)(2,1)}) %all-reduce.6.cloned.1.call-update) | async-done | bytes 131088 | tf_op jit(solution)/shard_map/psum | solution.py:20
  526.4 6.2 collective-permute-done.1
  533.7 3.0 fusion.83
  536.9 82.3 %all-gather.8.cloned.1.call-done = bf16[4096,512]{1,0:T(8,128)(2,1)} async-done(((bf16[128,512]{1,0:T(8,128)(2,1)}), bf16[4096,512]{1,0:T(8,128)(2,1)}) %all-gather.8.cloned.1.call-update) | async-done | bytes 4194320 | tf_op jit(solution)/shard_map/all_gather | solution.py:106
  619.1 87.2 %while.47 = (s32[]{:T(128)}, f32[4,4,128]{2,1,0:T(4,128)S(1)}, f32[4,4,128]{2,1,0:T(4,128)S(1)}, f32[4,4,128,64]{2,3,1,0:T(8,128)}, s32[8]{0:T(128)S(1)}, /*inde...) while((s32[]{:T(128)}, f32[4,4,128]{2,1,0:T(4,128)S(1)}, ...), condition=%wide.region_18.19_spmd.clone, body=%wide.region_15.18_spmd.clone.sunk | while | flops 282536576 | bytes 38933744 | solution.py:77
  621.9 2.7 fusion.197
  624.6 3.3 fusion.198
  632.8 2.7 fusion.197
  635.5 3.3 fusion.198
  643.7 2.7 fusion.197
  646.4 3.3 fusion.198
  654.6 2.7 fusion.197
  657.4 3.3 fusion.198
  665.5 2.7 fusion.197
  668.3 3.3 fusion.198
  676.4 2.7 fusion.197
  679.2 3.3 fusion.198
  687.3 2.7 fusion.197
  690.1 3.3 fusion.198
  698.2 2.7 fusion.197
  701.0 3.3 fusion.198
  707.5 3.1 fusion.97
  711.9 70.0 %all-reduce.8.cloned.1.call-done = bf16[128,512]{1,0:T(8,128)(2,1)} async-done(((bf16[128,512]{1,0:T(8,128)(2,1)}), bf16[128,512]{1,0:T(8,128)(2,1)}) %all-reduce.8.cloned.1.call-update) | async-done | bytes 131088 | tf_op jit(solution)/shard_map/psum | solution.py:20
  782.7 50.0 %all_gather.15 = bf16[4096,64]{1,0:T(8,128)(2,1)S(1)} all-gather(bf16[128,64]{1,0:T(8,128)(2,1)S(1)} %constant_dynamic-slice_fusion.3), channel_id=1, replica_groups=mesh['section'=8,'ctx'=32] {'ctx'}, dimensions={0}, use_global_device_ids=true | all-gather | bytes 540672 | tf_op jit(solution)/shard_map/all_gather | solution.py:127
  (479 shorter events, 125.7 us)
Async XLA Ops:
  7.2 2.1 copy-start
  7.2 95.5 %all-gather.4.cloned.1.call-start = ((), (), s32[]{:S(2)}) async-start(), calls=%async_computation | async-start | bytes 4325376 | tf_op jit(solution)/shard_map/all_gather | solution.py:106
  11.5 254.8 %all-reduce.4.cloned.1.call-start = ((), (), s32[]{:S(2)}) async-start(), calls=%async_computation.1 | async-start | bytes 262144 | tf_op jit(solution)/shard_map/psum | solution.py:20
  105.4 6.1 copy-start.10
  108.2 3.4 copy-start.1
  116.3 6.1 copy-start.10
  119.1 3.4 copy-start.1
  127.2 6.1 copy-start.10
  130.0 3.4 copy-start.1
  138.1 6.1 copy-start.10
  140.9 3.4 copy-start.1
  149.0 6.1 copy-start.10
  151.8 3.4 copy-start.1
  159.9 6.1 copy-start.10
  162.7 3.4 copy-start.1
  170.8 6.1 copy-start.10
  173.6 3.4 copy-start.1
  181.8 6.1 copy-start.10
  184.5 3.4 copy-start.1
  191.0 83.0 %copy-start.4 = (bf16[128,2048]{1,0:T(8,128)(2,1)S(1)}, bf16[128,2048]{1,0:T(8,128)(2,1)}, u32[]{:S(2)}) copy-start(bf16[128,2048]{1,0:T(8,128)(2,1)} %param.13) | copy-start | bytes 1572868
  194.2 0.8 copy-start.16
  196.2 165.0 %all-gather.6.cloned.1.call-start = ((), (), s32[]{:S(2)}) async-start(), calls=%async_computation.2 | async-start | bytes 4325376 | tf_op jit(solution)/shard_map/all_gather | solution.py:106
  266.3 258.5 %all-reduce.6.cloned.1.call-start = ((), (), s32[]{:S(2)}) async-start(), calls=%async_computation.3 | async-start | bytes 262144 | tf_op jit(solution)/shard_map/psum | solution.py:20
  266.3 7.7 collective-permute-start
  274.3 0.8 copy-start.7
  364.0 6.1 copy-start.12
  366.7 3.4 copy-start.2
  374.9 6.1 copy-start.12
  377.7 3.4 copy-start.2
  385.8 6.1 copy-start.12
  388.6 3.4 copy-start.2
  396.7 6.1 copy-start.12
  399.5 3.4 copy-start.2
  407.6 6.1 copy-start.12
  410.4 3.4 copy-start.2
  418.5 6.1 copy-start.12
  421.3 3.4 copy-start.2
  429.4 6.1 copy-start.12
  432.2 3.4 copy-start.2
  440.3 6.1 copy-start.12
  443.1 3.4 copy-start.2
  449.6 83.0 %copy-start.5 = (bf16[128,2048]{1,0:T(8,128)(2,1)S(1)}, bf16[128,2048]{1,0:T(8,128)(2,1)}, u32[]{:S(2)}) copy-start(bf16[128,2048]{1,0:T(8,128)(2,1)} %param.13) | copy-start | bytes 1572868
  454.8 164.3 %all-gather.8.cloned.1.call-start = ((), (), s32[]{:S(2)}) async-start(), calls=%async_computation.4 | async-start | bytes 4325376 | tf_op jit(solution)/shard_map/all_gather | solution.py:106
  524.8 257.0 %all-reduce.8.cloned.1.call-start = ((), (), s32[]{:S(2)}) async-start(), calls=%async_computation.5 | async-start | bytes 262144 | tf_op jit(solution)/shard_map/psum | solution.py:20
  524.9 7.7 collective-permute-start.1
  532.9 0.8 copy-start.6
  621.9 6.1 copy-start.8
  624.6 3.4 copy-start.3
  632.8 6.1 copy-start.8
  635.5 3.4 copy-start.3
  643.7 6.1 copy-start.8
  646.4 3.4 copy-start.3
  654.6 6.1 copy-start.8
  657.3 3.4 copy-start.3
  665.5 6.1 copy-start.8
  668.2 3.4 copy-start.3
  676.4 6.1 copy-start.8
  679.2 3.4 copy-start.3
  687.3 6.1 copy-start.8
  690.1 3.4 copy-start.3
  698.2 6.1 copy-start.8
  701.0 3.4 copy-start.3
  707.5 4.4 copy-start.17
  710.6 123.1 %copy-start.15 = (bf16[128,2048]{1,0:T(8,128)(2,1)}, bf16[128,2048]{1,0:T(8,128)(2,1)S(1)}, u32[]{:S(2)}) copy-start(bf16[128,2048]{1,0:T(8,128)(2,1)S(1)} %get-tuple-element.350) | copy-start | bytes 1572868
  (25 other events, 19.9 us)
Sparse Core Ops, SparseCore 0:
  11.6 91.0 all-gather.3
  196.3 69.8 all-reduce.3
  269.4 91.7 all-gather.5
  454.9 69.8 all-reduce.5
  527.4 91.6 all-gather.7
  712.0 69.8 all-reduce.7
where the time goes:
time: 843 us; the launch traced here: 841 us
  waiting for transfers between devices  475 us (56%)
  matrix products  118 us (14%)
  other arithmetic  90.8 us (11%)
  local copies, waits for them, and re-layouts  72.7 us (9%)
  blocking collectives  50 us (6%)
  loops' own time  16.9 us (2%)
  between operations  14.4 us (2%)
    all_gather x3, waiting for transfers between devices, body(): lax.all_gather(cache_local, 'ctx', axis=0, tiled=True)  252 us
    psum x3, waiting for transfers between devices, broadcast(): return lax.psum(kept, axis)  210 us
    reduce_sum x24, other arithmetic, online_update(): jnp.sum(probs, axis=-1)  79.8 us
    dot_general x24, matrix products, online_update(): jnp.einsum('igrd,jgd->grij', query_rows, key_rows, preferred_element_type...  65.9 us
    all_gather x1, blocking collectives, body(): piece = lax.all_gather(mine, 'ctx', axis=0, tiled=True)  50 us
    dynamic_slice x72, local copies, waits for them, and re-layouts, attend_piece(): lax.scan(one_block, loop_state, (blocks, jnp.arange(number, dtype=jnp.int...  45.8 us
    dot_general x24, matrix products, online_update(): jnp.einsum('grij,jgd->grid', probs.astype(jnp.bfloat16), value_rows, pref...  27.7 us
    while x168, local copies, waits for them, and re-layouts  20.7 us
  transfers between devices with their start and end apart: 8, of which 8 were waited for; matrix products, arithmetic and copies ran while one was open for 1% of the time, Pallas kernels for 0%

commit v1 on v0

v1 whole, which is shorter than its diff:
```python
import jax
import jax.numpy as jnp
from jax import lax
from jax.experimental import pallas as pl
from jax.experimental.pallas import tpu as pltpu
from jax.sharding import PartitionSpec as P

BF16, F32 = jnp.bfloat16, jnp.float32
MESH = pl.DeviceIdType.MESH
WIDTH = 2048
ROWS = 128
HEADS = 16
KV_HEADS = 4
HEAD = 64
ITERS = 3
EPS = 1e-05
NEG = -1e30
QSCALE = HEAD**-0.5 * 1.4426950408889634


def normalize(rows, gain):
    wide = rows.astype(F32)
    factor = lax.rsqrt(jnp.mean(wide * wide, axis=-1, keepdims=True) + EPS)
    return (wide * factor * gain.astype(F32)).astype(BF16)


def kernel(
    embeds, q_weight, out_weight, kv_weight, norm_gain, kv_gain, block_slot,
    layer_out, decode,
    wq, wo, wkv, hid, xs, kv, qst, qbuf, mst, mbuf, hout, ka, kb, vt, mx, acc,
    fx, grid, pick, land, inv,
    load_sem, kvd_s, kvd_r, sib_s, sib_r, q_s, q_r, m_s, m_r, h_s, h_r, ks_s, ks_r,
    f1_s, f1_r, f2_s, f2_r, f3_s, f3_r,
):
    s, c = lax.axis_index("section"), lax.axis_index("ctx")
    x_lo, y = s // 4, s % 4
    z, xh, core = c // 4, (c // 2) % 2, c % 2
    xc = c % 4
    top = s == 7
    sib = z * 4 + xh * 2 + (1 - core)

    loads = [
        pltpu.make_async_copy(src, dst, load_sem.at[i])
        for i, (src, dst) in enumerate(
            ((embeds, hid[0]), (kv_weight, wkv), (q_weight.at[0], wq), (out_weight.at[0], wo))
        )
    ]
    for copy in loads:
        copy.start()

    barrier = pltpu.get_barrier_semaphore()

    def greet(section, ctx):
        pl.semaphore_signal(barrier, inc=1, device_id=(section, ctx), device_id_type=MESH)

    for d in range(1, 8):
        greet((s + d) % 8, c)
    for dz in range(8):
        for dx in range(2):
            if dz or dx:
                greet(s, ((z + dz) % 8) * 4 + ((xh + dx) % 2) * 2 + core)
    greet(s, sib)
    greet(s, z * 4 + (1 - xh) * 2 + (1 - core))
    pl.semaphore_wait(barrier, 7 + 15 + 2)

    def send(src, dst, ssem, rsem, section, ctx):
        return pltpu.make_async_remote_copy(
            src_ref=src, dst_ref=dst, send_sem=ssem, recv_sem=rsem,
            device_id=(section, ctx), device_id_type=MESH,
        )

    def kv_out(t, z2, x2):
        return send(kv[t].at[c], kv[t].at[c], kvd_s.at[t, z2 * 2 + x2],
                    kvd_r.at[t, z * 2 + xh], s, z2 * 4 + x2 * 2 + core)

    def kv_in(t, z2, x2):
        b = z2 * 4 + x2 * 2 + core
        return send(kv[t].at[b], kv[t].at[b], kvd_s.at[t, z2 * 2 + x2],
                    kvd_r.at[t, z2 * 2 + x2], s, sib)

    def sib_out(t, z2, x2):
        b = z2 * 4 + x2 * 2 + core
        return send(kv[t].at[b], kv[t].at[b], sib_s.at[t, z2 * 2 + x2],
                    sib_r.at[t, z2 * 2 + x2], s, sib)

    def sib_in(t, z2, x2):
        b = z2 * 4 + x2 * 2 + 1 - core
        return send(kv[t].at[b], kv[t].at[b], sib_s.at[t, z2 * 2 + x2],
                    sib_r.at[t, z2 * 2 + x2], s, sib)

    def q_out(t, j):
        return send(qst[t].at[j], qbuf[t].at[y], q_s.at[t, j], q_r.at[t, y], x_lo * 4 + j, c)

    def q_in(t, j):
        return send(qst[t].at[j], qbuf[t].at[j], q_s.at[t, j], q_r.at[t, j], x_lo * 4 + j, c)

    def m_out(t, i):
        return send(mst[t].at[i], mbuf[t].at[y], m_s.at[t, i], m_r.at[t, y], x_lo * 4 + i, c)

    def m_in(t, j):
        return send(mst[t].at[j], mbuf[t].at[j], m_s.at[t, j], m_r.at[t, j], x_lo * 4 + j, c)

    def h_out(t):
        return send(hout[t], hid[t + 1], h_s.at[t], h_r.at[t], (s + 1) % 8, c)

    def ks_out(t, s2):
        dst = kv[t].at[c] if t < ITERS else fx
        return send(xs[t].at[s2 % 4], dst, ks_s.at[t - 1, s2], ks_r.at[t - 1], s2, c)

    def f1_out(i):
        return send(fx.at[pl.ds(16 * i, 16)], grid.at[xc, z], f1_s.at[i], f1_r.at[z], s, i * 4 + xc)

    def f1_in(i):
        return send(fx.at[pl.ds(0, 16)], grid.at[xc, i], f1_s.at[i], f1_r.at[i], s, i * 4 + xc)

    def f2_out(d):
        other = (xc + d) % 4
        return send(grid.at[xc], grid.at[xc], f2_s.at[d], f2_r.at[d], s, z * 4 + other)

    def f2_in(d):
        other = (xc + 4 - d) % 4
        return send(grid.at[other], grid.at[other], f2_s.at[d], f2_r.at[d], s, z * 4 + other)

    def f3_out(i):
        return send(pick.at[i], land.at[z], f3_s.at[i], f3_r.at[z], s, i * 4 + xc)

    def f3_in(i):
        return send(pick.at[i], land.at[i], f3_s.at[i], f3_r.at[i], s, i * 4 + xc)

    lane = lax.broadcasted_iota(jnp.int32, (ROWS, 128), 1)

    def project(hidden, t):
        normed = normalize(hidden, kv_gain[...])
        rows = jnp.dot(normed, wkv[...], preferred_element_type=F32)
        for j in range(KV_HEADS):
            a, half = 128 * (j // 2), j % 2
            keys, values = rows[:, a:a + 128], rows[:, 256 + a:384 + a]
            if half == 0:
                both = jnp.where(lane < HEAD, keys, pltpu.roll(values, HEAD, 1))
            else:
                both = jnp.where(lane < HEAD, pltpu.roll(keys, HEAD, 1), values)
            xs[t][j] = both.astype(BF16)

    def spread(t):
        sib_out(t, z, xh).start()
        kv_out(t, z, 1 - xh).start()
        for d in range(1, 8):
            @pl.when(z + d < 8)
            def _():
                for x2 in range(2):
                    kv_out(t, z + d, x2).start()

    def spread_done(t):
        sib_out(t, z, xh).wait_send()
        kv_out(t, z, 1 - xh).wait_send()
        for d in range(1, 8):
            @pl.when(z + d < 8)
            def _():
                for x2 in range(2):
                    kv_out(t, z + d, x2).wait_send()

    def relay_early(t):
        for z2 in range(7):
            @pl.when(z2 < z)
            def _():
                for x2 in range(2):
                    kv_in(t, z2, x2).wait_recv()
                    sib_out(t, z2, x2).start()

    def relay_own(t):
        kv_in(t, z, 1 - xh).wait_recv()
        sib_out(t, z, 1 - xh).start()

    def relay_done(t):
        sib_out(t, z, 1 - xh).wait_send()
        for z2 in range(7):
            @pl.when(z2 < z)
            def _():
                for x2 in range(2):
                    sib_out(t, z2, x2).wait_send()

    def queries(t):
        normed = normalize(hid[t][...], norm_gain[...])
        for j in range(KV_HEADS):
            rows = jnp.dot(normed, wq[:, 256 * j:256 * j + 256], preferred_element_type=F32)
            rows = (rows * QSCALE).astype(BF16)

            @pl.when(y == j)
            def _():
                for p in range(2):
                    qbuf[t][j, p] = rows[:, 128 * p:128 * p + 128]

            @pl.when(y != j)
            def _():
                for p in range(2):
                    qst[t][j, p] = rows[:, 128 * p:128 * p + 128]
                q_out(t, j).start()

    key_row = lax.broadcasted_iota(jnp.int32, (128, 512), 0)
    key_lane = lax.broadcasted_iota(jnp.int32, (512, 128), 1)

    def prepare(t, z2):
        x = kv[t][pl.ds(z2 * 4, 4)].reshape(512, 128).astype(F32)
        r = pltpu.roll(x, HEAD, 1)
        at = pl.ds(pl.multiple_of(z2 * 512, 512), 512)
        ka[at, :] = jnp.where(key_lane < HEAD, x, 0.0).astype(BF16)
        kb[at, :] = jnp.where(key_lane < HEAD, 0.0, r).astype(BF16)
        vt[:, at] = jnp.where(key_row < HEAD, r.T, 1.0).astype(BF16)

    def unit(t, z2, masked):
        at = pl.ds(pl.multiple_of(z2 * 512, 512), 512)
        qq = qbuf[t][...].reshape(1024, 128)
        for h, keys in enumerate((ka, kb)):
            scores = lax.dot_general(
                keys[at, :], qq, (((1,), (1,)), ((), ())), preferred_element_type=F32
            )
            if masked:
                kpos = lax.broadcasted_iota(jnp.int32, (512, 1024), 0)
                qpos = lax.broadcasted_iota(jnp.int32, (512, 1024), 1) % ROWS + xc * ROWS
                scores = jnp.where(kpos <= qpos, scores, NEG)
            old = mx[h]
            new = jnp.maximum(old, jnp.max(scores, axis=0, keepdims=True))
            decay = jnp.exp2(old - new)
            mx[h] = new
            probs = jnp.exp2(scores - new).astype(BF16)
            acc[h] = acc[h] * decay + jnp.dot(vt[0:72, at], probs, preferred_element_type=F32)

    def attend(t):
        mx[...] = jnp.full(mx.shape, NEG, F32)
        acc[...] = jnp.zeros(acc.shape, F32)
        for z2 in range(7):
            @pl.when(z2 < z)
            def _():
                for x2 in range(2):
                    sib_in(t, z2, x2).wait_recv()
                prepare(t, z2)

        def body(z2, carry):
            unit(t, z2, False)
            return carry

        lax.fori_loop(0, z, body, 0)
        sib_in(t, z, 0).wait_recv()
        sib_in(t, z, 1).wait_recv()
        prepare(t, z)
        unit(t, z, True)
        for i in range(4):
            for p in range(2):
                at = slice((2 * i + p) * 128, (2 * i + p) * 128 + 128)
                halves = [acc[h, 0:HEAD, at] / acc[h, HEAD:HEAD + 1, at] for h in range(2)]
                rows = jnp.concatenate(halves, axis=0).T.astype(BF16)

                @pl.when(y == i)
                def _():
                    mbuf[t][i, :, 128 * p:128 * p + 128] = rows

                @pl.when(y != i)
                def _():
                    mst[t][i, :, 128 * p:128 * p + 128] = rows

            @pl.when(y != i)
            def _():
                m_out(t, i).start()

    def finish(t, out):
        for j in range(4):
            @pl.when(y != j)
            def _():
                m_in(t, j).wait_recv()
        mixed = jnp.concatenate([mbuf[t][j] for j in range(4)], axis=1)
        for n in range(4):
            at = slice(512 * n, 512 * n + 512)
            grown = jnp.dot(mixed, wo[:, at], preferred_element_type=F32)
            out[:, at] = (hid[t][:, at].astype(F32) + grown).astype(BF16)

    loads[0].wait()
    loads[1].wait()
    project(hid[0][...], 0)
    kv[0][c] = xs[0][y]
    spread(0)
    loads[2].wait()
    queries(0)

    @pl.when(s == 0)
    def _():
        for t in range(1, ITERS):
            hid[t][...] = hid[0][...]

    def invert(b, found):
        slot = block_slot[b]
        return tuple(jnp.where(slot == i * 4 + xc, b, f) for i, f in enumerate(found))

    found = lax.fori_loop(0, 32, invert, (jnp.int32(0),) * 8)
    for i in range(8):
        inv[i] = found[i]

    relay_own(0)
    relay_early(0)
    for t in range(ITERS):
        for j in range(4):
            @pl.when(y != j)
            def _():
                q_in(t, j).wait_recv()
        attend(t)
        if t == 0:
            loads[3].wait()
        last = t + 1 == ITERS
        finish(t, layer_out.at[0] if last else hout[t])
        if not last:
            @pl.when(s < 7)
            def _():
                h_out(t).start()

        @pl.when(top)
        def _():
            project(layer_out[0] if last else hout[t][...], t + 1)
            for s2 in range(7):
                ks_out(t + 1, s2).start()
            if last:
                fx[...] = xs[t + 1][3]
            else:
                kv[t + 1][c] = xs[t + 1][3]

        @pl.when(s < 7)
        def _():
            ks_out(t + 1, 0).wait_recv()

        if not last:
            spread(t + 1)
            relay_early(t + 1)

            @pl.when(s > 0)
            def _():
                h_out(t).wait_recv()

            queries(t + 1)
            relay_own(t + 1)

    for i in range(8):
        @pl.when(z != i)
        def _():
            f1_out(i).start()
    grid[xc, z] = fx[pl.ds(pl.multiple_of(z * 16, 16), 16), :]
    for i in range(8):
        @pl.when(z != i)
        def _():
            f1_in(i).wait_recv()
    for d in range(1, 4):
        f2_out(d).start()
    for d in range(1, 4):
        f2_in(d).wait_recv()
    for i in range(8):
        b = inv[i]
        rows = grid[b % 4, b // 4]

        @pl.when(z != i)
        def _():
            pick[i] = rows
            f3_out(i).start()

        @pl.when(z == i)
        def _():
            land[i] = rows
    for i in range(8):
        @pl.when(z != i)
        def _():
            f3_in(i).wait_recv()
    rows = land[...].reshape(ROWS, 128)

    @pl.when(x_lo == 0)
    def _():
        decode[0] = rows[:, :HEAD]

    @pl.when(x_lo != 0)
    def _():
        decode[0] = rows[:, HEAD:]

    for t in range(ITERS):
        spread_done(t)
        relay_done(t)
        for j in range(4):
            @pl.when(y != j)
            def _():
                q_out(t, j).wait_send()
                m_out(t, j).wait_send()
        if t + 1 < ITERS:
            @pl.when(s < 7)
            def _():
                h_out(t).wait_send()

        @pl.when(top)
        def _():
            for s2 in range(7):
                ks_out(t + 1, s2).wait_send()
    for i in range(8):
        @pl.when(z != i)
        def _():
            f1_out(i).wait_send()
            f3_out(i).wait_send()
    for d in range(1, 4):
        f2_out(d).wait_send()


def body(embeds, q_weight, out_weight, norm_gain, kv_weight, kv_gain, block_slot):
    vmem = pl.BlockSpec(memory_space=pltpu.VMEM)
    hbm = pl.BlockSpec(memory_space=pl.ANY)
    dma = pltpu.SemaphoreType.DMA
    return pl.pallas_call(
        kernel,
        out_shape=(
            jax.ShapeDtypeStruct((1, ROWS, WIDTH), BF16),
            jax.ShapeDtypeStruct((1, ROWS, HEAD), BF16),
        ),
        in_specs=[hbm, hbm, hbm, hbm, vmem, vmem, pl.BlockSpec(memory_space=pltpu.SMEM)],
        out_specs=(vmem, vmem),
        scratch_shapes=[
            pltpu.VMEM((WIDTH, 1024), BF16),
            pltpu.VMEM((1024, WIDTH), BF16),
            pltpu.VMEM((WIDTH, 512), BF16),
            ITERS * (pltpu.VMEM((ROWS, WIDTH), BF16),),
            (ITERS + 1) * (pltpu.VMEM((4, ROWS, 128), BF16),),
            ITERS * (pltpu.VMEM((32, ROWS, 128), BF16),),
            ITERS * (pltpu.VMEM((4, 2, ROWS, 128), BF16),),
            ITERS * (pltpu.VMEM((4, 2, ROWS, 128), BF16),),
            ITERS * (pltpu.VMEM((4, ROWS, 256), BF16),),
            ITERS * (pltpu.VMEM((4, ROWS, 256), BF16),),
            (ITERS - 1) * (pltpu.VMEM((ROWS, WIDTH), BF16),),
            pltpu.VMEM((4096, 128), BF16),
            pltpu.VMEM((4096, 128), BF16),
            pltpu.VMEM((128, 4096), BF16),
            pltpu.VMEM((2, 1, 1024), F32),
            pltpu.VMEM((2, 72, 1024), F32),
            pltpu.VMEM((ROWS, 128), BF16),
            pltpu.VMEM((4, 8, 16, 128), BF16),
            pltpu.VMEM((8, 16, 128), BF16),
            pltpu.VMEM((8, 16, 128), BF16),
            pltpu.SMEM((8,), jnp.int32),
            dma((4,)),
            dma((ITERS, 16)), dma((ITERS, 16)), dma((ITERS, 16)), dma((ITERS, 16)),
            dma((ITERS, 4)), dma((ITERS, 4)), dma((ITERS, 4)), dma((ITERS, 4)),
            dma((ITERS,)), dma((ITERS,)), dma((ITERS, 8)), dma((ITERS,)),
            dma((8,)), dma((8,)), dma((4,)), dma((4,)), dma((8,)), dma((8,)),
        ],
        compiler_params=pltpu.CompilerParams(
            collective_id=0, has_side_effects=True, vmem_limit_bytes=56 << 20
        ),
        cost_estimate=pl.CostEstimate(
            flops=20 * 10**9, bytes_accessed=12 * 2**20, transcendentals=10**7
        ),
    )(embeds, q_weight, out_weight, kv_weight, norm_gain, kv_gain.reshape(1, WIDTH), block_slot)


def solution(mesh):
    return jax.shard_map(
        body,
        mesh=mesh,
        in_specs=(
            P("ctx", None),
            P("section", None, None),
            P("section", None, None),
            P("section", None),
            P(),
            P(),
            P(),
        ),
        out_specs=(P("section", "ctx", None), P("ctx", None, "section")),
        check_vma=False,
    )
```

time: 843 us -> 167 us (0.20)
  waiting for transfers between devices: 475 us -> 0 us
  Pallas kernels: 0 us -> 161 us
  matrix products: 118 us -> 0 us
  other arithmetic: 90.8 us -> 0 us
  local copies, waits for them, and re-layouts: 72.7 us -> 4.62 us
  blocking collectives: 50 us -> 0 us
  loops' own time: 16.9 us -> 0 us
  between operations: 14.4 us -> 0.64 us
    all_gather x3 -> x0, waiting for transfers between devices: 252 us -> none  [body(): lax.all_gather(cache_local, 'ctx', axis=0, tiled=True)]
    psum x3 -> x0, waiting for transfers between devices: 210 us -> none  [broadcast(): return lax.psum(kept, axis)]
    pallas_call x0 -> x1, Pallas kernels: none -> 161 us  [body(): pl.pallas_call(kernel, out_shape=(jax.ShapeDtypeStruct((1, ROWS, WIDTH),...]
    dot_general x58 -> x0, matrix products: 118 us -> none  [the longest x24 65.9 us: online_update(): jnp.einsum('igrd,jgd->grij', query_rows, key_rows, preferred_element_type...]
    reduce_sum x27 -> x0, other arithmetic: 81.6 us -> none  [the longest x24 79.8 us: online_update(): jnp.sum(probs, axis=-1)]
    all_gather x1 -> x0, blocking collectives: 50 us -> none  [body(): piece = lax.all_gather(mine, 'ctx', axis=0, tiled=True)]
    dynamic_slice x73 -> x0, local copies, waits for them, and re-layouts: 46.6 us -> none  [the longest x72 45.8 us: attend_piece(): lax.scan(one_block, loop_state, (blocks, jnp.arange(number, dtype=jnp.int...]
    while x168 -> x0, local copies, waits for them, and re-layouts: 20.7 us -> none
  transfers between devices with their start and end apart: 8 -> 0, of which waited for: 8 -> 0; matrix products, arithmetic and copies ran while one was open for 1% -> 0% of each run, Pallas kernels for 0% -> 0%
where the time goes in v1:
time: 167 us; the launch traced here: 166 us
  Pallas kernels  161 us (96%)
  local copies, waits for them, and re-layouts  4.62 us (3%)
    pallas_call x1, Pallas kernels, body(): pl.pallas_call(kernel, out_shape=(jax.ShapeDtypeStruct((1, ROWS, WIDTH),...  161 us

profile of v1, /device:TPU:1, one launch (start us, length us, event | category | flops | bytes accessed | tf_op | source)
XLA Modules:
  0.0 166.4 jit_solution(5967820113752046967)
XLA Ops:
  0.6 1.3 reshape.7.kv_gain
  1.9 161.1 %shard_map.86 = (bf16[1,128,2048]{2,1,0:T(8,128)(2,1)}, bf16[1,128,64]{2,1,0:T(8,128)(2,1)}) custom-call(bf16[128,2048]{1,0:T(8,128)(2,1)} %embeds.1, bf16[1,2048,1024]{2,1,0:T(8,128)(2,1)} %q_weight.1, bf16[1,1024,2048]{2,1,0:T(8,128)(2,1)} %out_weight.1, bf16[2048,512]{1,0:T(8,128)(2,1)} %kv_weight.1, bf16[1,2048]{1,0:T(2,128)(2,1)} %norm_gain.1, ...), custom_call_target="tpu_custom_call" | custom-call | flops 20000000000 | bytes 12582912 | tf_op jit(solution)/shard_map/pallas_call | solution.py:408
  163.0 1.4 copy.9
  164.5 1.9 %copy.11 = bf16[1,128,2048]{2,1,0:T(8,128)(2,1)} copy(bf16[1,128,2048]{2,1,0:T(8,128)(2,1)} %get-tuple-element.6) | data formatting | bytes 1048576

commit v2 on v1

v2 whole, which is shorter than its diff:
```python
import jax
import jax.numpy as jnp
from jax import lax
from jax.experimental import pallas as pl
from jax.experimental.pallas import tpu as pltpu
from jax.sharding import PartitionSpec as P

BF16, F32 = jnp.bfloat16, jnp.float32
MESH = pl.DeviceIdType.MESH
WIDTH = 2048
ROWS = 128
HEADS = 16
KV_HEADS = 4
HEAD = 64
ITERS = 3
EPS = 1e-05
NEG = -1e30
QSCALE = HEAD**-0.5 * 1.4426950408889634


def normalize(rows, gain):
    wide = rows.astype(F32)
    factor = lax.rsqrt(jnp.mean(wide * wide, axis=-1, keepdims=True) + EPS)
    return (wide * factor * gain.astype(F32)).astype(BF16)


def kernel(
    embeds, q_weight, out_weight, kv_weight, norm_gain, kv_gain, block_slot,
    layer_out, decode,
    wq, wo, wkv, hid, xs, xf, kv, qst, qbuf, mst, mbuf, hout, ka, kb, vt, mx, acc, qacc, fin,
    load_sem, kvd_s, kvd_r, sib_s, sib_r, q_s, q_r, m_s, m_r, h_s, h_r, ks_s, ks_r,
    fin_s, fin_r,
):
    s, c = lax.axis_index("section"), lax.axis_index("ctx")
    x_lo, y = s // 4, s % 4
    z, xh, core = c // 4, (c // 2) % 2, c % 2
    xc = c % 4
    top = s == 7
    sib = z * 4 + xh * 2 + (1 - core)

    rows0 = hid[0]
    loads = [
        pltpu.make_async_copy(src, dst, load_sem.at[i])
        for i, (src, dst) in enumerate(
            ((embeds, rows0), (kv_weight, wkv), (q_weight.at[0], wq), (out_weight.at[0], wo))
        )
    ]
    for copy in loads:
        copy.start()

    barrier = pltpu.get_barrier_semaphore()

    def greet(section, ctx):
        pl.semaphore_signal(barrier, inc=1, device_id=(section, ctx), device_id_type=MESH)

    for d in range(1, 8):
        greet((s + d) % 8, c)
    for d in range(1, 32):
        greet(s, (c + d) % 32)
    pl.semaphore_wait(barrier, 7 + 31)

    def send(src, dst, ssem, rsem, section, ctx):
        return pltpu.make_async_remote_copy(
            src_ref=src, dst_ref=dst, send_sem=ssem, recv_sem=rsem,
            device_id=(section, ctx), device_id_type=MESH,
        )

    def kv_out(t, d, x2):
        return send(kv[t][0].at[xc], kv[t][d].at[xc], kvd_s.at[t, d * 2 + x2],
                    kvd_r.at[t, d * 2 + xh], s, (z + d) * 4 + x2 * 2 + core)

    def kv_in(t, d, x2):
        b = x2 * 2 + core
        return send(kv[t][d].at[b], kv[t][d].at[b], kvd_s.at[t, d * 2 + x2],
                    kvd_r.at[t, d * 2 + x2], s, sib)

    def sib_out(t, d, x2):
        b = x2 * 2 + core
        return send(kv[t][d].at[b], kv[t][d].at[b], sib_s.at[t, d * 2 + x2],
                    sib_r.at[t, d * 2 + x2], s, sib)

    def sib_in(t, d, x2):
        b = x2 * 2 + 1 - core
        return send(kv[t][d].at[b], kv[t][d].at[b], sib_s.at[t, d * 2 + x2],
                    sib_r.at[t, d * 2 + x2], s, sib)

    def q_out(t, j):
        return send(qst[t].at[j], qbuf[t].at[y], q_s.at[t, j], q_r.at[t, y], x_lo * 4 + j, c)

    def q_in(t, j):
        return send(qst[t].at[j], qbuf[t].at[j], q_s.at[t, j], q_r.at[t, j], x_lo * 4 + j, c)

    def m_out(t, i):
        return send(mst[t].at[i], mbuf[t].at[y], m_s.at[t, i], m_r.at[t, y], x_lo * 4 + i, c)

    def m_in(t, j):
        return send(mst[t].at[j], mbuf[t].at[j], m_s.at[t, j], m_r.at[t, j], x_lo * 4 + j, c)

    def h_out(t, n):
        return send(hout[t][n], hid[t + 1][n], h_s.at[t, n], h_r.at[t, n], (s + 1) % 8, c)

    def ks_out(t, s2):
        if t < ITERS:
            return send(xs[t].at[s2 % 4], kv[t][0].at[xc], ks_s.at[t - 1, s2], ks_r.at[t - 1], s2, c)
        return send(xf.at[s2], fin.at[c], ks_s.at[t - 1, s2], ks_r.at[t - 1], s2, c)

    def fin_out(d):
        return send(fin.at[c], fin.at[c], fin_s.at[d], fin_r.at[d], s, (c + d) % 32)

    def fin_in(d):
        b = (c + 32 - d) % 32
        return send(fin.at[b], fin.at[b], fin_s.at[d], fin_r.at[d], s, b)

    lane = lax.broadcasted_iota(jnp.int32, (ROWS, 128), 1)

    def cache_rows(hidden):
        normed = normalize(hidden, kv_gain[...].reshape(1, WIDTH))
        return jnp.dot(normed, wkv[...], preferred_element_type=F32)

    def project(hidden, t):
        rows = cache_rows(hidden)
        for j in range(KV_HEADS):
            a, half = 128 * (j // 2), j % 2
            keys, values = rows[:, a:a + 128], rows[:, 256 + a:384 + a]
            if half == 0:
                both = jnp.where(lane < HEAD, keys, pltpu.roll(values, HEAD, 1))
            else:
                both = jnp.where(lane < HEAD, pltpu.roll(keys, HEAD, 1), values)
            xs[t][j] = both.astype(BF16)

    def project_last(hidden):
        rows = cache_rows(hidden)
        low = lane[:HEAD] < HEAD
        for s2 in range(8):
            a = 128 * (s2 // 2)
            upper, lower = rows[:HEAD, a:a + 128], rows[HEAD:, a:a + 128]
            if s2 % 2 == 0:
                both = jnp.where(low, upper, pltpu.roll(lower, HEAD, 1))
            else:
                both = jnp.where(low, pltpu.roll(upper, HEAD, 1), lower)
            xf[s2] = both.astype(BF16)

    def spread(t):
        sib_out(t, 0, xh).start()
        kv_out(t, 0, 1 - xh).start()
        for d in range(1, 8):
            @pl.when(z + d < 8)
            def _():
                for x2 in range(2):
                    kv_out(t, d, x2).start()

    def spread_done(t):
        sib_out(t, 0, xh).wait_send()
        kv_out(t, 0, 1 - xh).wait_send()
        for d in range(1, 8):
            @pl.when(z + d < 8)
            def _():
                for x2 in range(2):
                    kv_out(t, d, x2).wait_send()

    def relay(t, d):
        for x2 in range(2):
            kv_in(t, d, x2).wait_recv()
            sib_out(t, d, x2).start()

    def relay_own(t):
        kv_in(t, 0, 1 - xh).wait_recv()
        sib_out(t, 0, 1 - xh).start()

    def relay_done(t):
        sib_out(t, 0, 1 - xh).wait_send()
        for d in range(1, 8):
            @pl.when(d <= z)
            def _():
                for x2 in range(2):
                    sib_out(t, d, x2).wait_send()

    def place_queries(t, j, rows):
        @pl.when(y == j)
        def _():
            for p in range(2):
                qbuf[t][j, p] = rows[:, 128 * p:128 * p + 128]

        @pl.when(y != j)
        def _():
            for p in range(2):
                qst[t][j, p] = rows[:, 128 * p:128 * p + 128]
            q_out(t, j).start()

    def first_queries():
        normed = normalize(rows0[...], norm_gain[...])
        for j in range(KV_HEADS):
            rows = jnp.dot(normed, wq[:, 256 * j:256 * j + 256], preferred_element_type=F32)
            place_queries(0, j, (rows * QSCALE).astype(BF16))

    def queries(t):
        squares = jnp.zeros((ROWS, 1), F32)
        for n in range(4):
            @pl.when(s > 0)
            def _():
                h_out(t - 1, n).wait_recv()

            at = slice(512 * n, 512 * n + 512)
            wide = hid[t][n][...].astype(F32)
            squares += jnp.sum(wide * wide, axis=-1, keepdims=True)
            gained = (wide * norm_gain[:, at].astype(F32)).astype(BF16)
            for j in range(KV_HEADS):
                cols = slice(256 * j, 256 * j + 256)
                part = jnp.dot(gained, wq[at, cols], preferred_element_type=F32)
                if n == 0:
                    qacc[:, cols] = part
                elif n < 3:
                    qacc[:, cols] += part
                else:
                    factor = lax.rsqrt(squares / WIDTH + EPS) * QSCALE
                    place_queries(t, j, ((qacc[:, cols] + part) * factor).astype(BF16))

    key_row = lax.broadcasted_iota(jnp.int32, (128, 512), 0)
    key_lane = lax.broadcasted_iota(jnp.int32, (512, 128), 1)

    def prepare(t, d):
        for x2 in range(2):
            sib_in(t, d, x2).wait_recv()
        x = kv[t][d][...].reshape(512, 128).astype(F32)
        r = pltpu.roll(x, HEAD, 1)
        at = slice(512 * d, 512 * d + 512)
        ka[at, :] = jnp.where(key_lane < HEAD, x, 0.0).astype(BF16)
        kb[at, :] = jnp.where(key_lane < HEAD, 0.0, r).astype(BF16)
        vt[:, at] = jnp.where(key_row < HEAD, r.T, 1.0).astype(BF16)

    def unit(t, d, masked):
        at = pl.ds(pl.multiple_of(d * 512, 512), 512)
        qq = qbuf[t][...].reshape(1024, 128)
        for h, keys in enumerate((ka, kb)):
            scores = lax.dot_general(
                keys[at, :], qq, (((1,), (1,)), ((), ())), preferred_element_type=F32
            )
            if masked:
                kpos = lax.broadcasted_iota(jnp.int32, (512, 1024), 0)
                qpos = lax.broadcasted_iota(jnp.int32, (512, 1024), 1) % ROWS + xc * ROWS
                scores = jnp.where(kpos <= qpos, scores, NEG)
            scores = scores.reshape(64, 8, 1024)
            top8 = jnp.max(scores, axis=0)
            for k in (4, 2, 1):
                top8 = jnp.maximum(top8, pltpu.roll(top8, k, 0))
            old = mx[h]
            new = jnp.maximum(old, top8)
            decay = jnp.exp2(old - new)
            mx[h] = new
            probs = jnp.exp2(scores - new[None]).astype(BF16).reshape(512, 1024)
            grown = jnp.dot(vt[0:72, at], probs, preferred_element_type=F32)
            acc[h] = (acc[h].reshape(9, 8, 1024) * decay[None]).reshape(72, 1024) + grown

    def wait_queries(t):
        for j in range(4):
            @pl.when(y != j)
            def _():
                q_in(t, j).wait_recv()

    def start_state():
        mx[...] = jnp.full(mx.shape, NEG, F32)
        acc[...] = jnp.zeros(acc.shape, F32)

    def first_units():
        start_state()
        relay_own(0)
        prepare(0, 0)

        @pl.when(z > 0)
        def _():
            relay(0, 1)

        wait_queries(0)
        unit(0, 0, True)

        def step(d, carry):
            for near in range(1, 8):
                @pl.when(d == near)
                def _():
                    if near < 7:
                        @pl.when(near < z)
                        def _():
                            relay(0, near + 1)

                    prepare(0, near)

            unit(0, d, False)
            return carry

        lax.fori_loop(1, z + 1, step, 0)

    def units(t):
        start_state()
        for d in range(7, 0, -1):
            @pl.when(d <= z)
            def _():
                prepare(t, d)

        wait_queries(t)

        def step(d, carry):
            unit(t, d, False)
            return carry

        lax.fori_loop(1, z + 1, step, 0)
        prepare(t, 0)
        unit(t, 0, True)

    def send_mixed(t):
        for i in range(4):
            for p in range(2):
                at = slice((2 * i + p) * 128, (2 * i + p) * 128 + 128)
                halves = [acc[h, 0:HEAD, at] / acc[h, HEAD:HEAD + 1, at] for h in range(2)]
                rows = jnp.concatenate(halves, axis=0).T.astype(BF16)

                @pl.when(y == i)
                def _():
                    mbuf[t][i, :, 128 * p:128 * p + 128] = rows

                @pl.when(y != i)
                def _():
                    mst[t][i, :, 128 * p:128 * p + 128] = rows

            @pl.when(y != i)
            def _():
                m_out(t, i).start()

    def finish(t):
        for j in range(4):
            @pl.when(y != j)
            def _():
                m_in(t, j).wait_recv()
        mixed = jnp.concatenate([mbuf[t][j] for j in range(4)], axis=1)
        for n in range(4):
            at = slice(512 * n, 512 * n + 512)
            grown = jnp.dot(mixed, wo[:, at], preferred_element_type=F32)
            before = rows0[:, at] if t == 0 else hid[t][n][...]
            out = (before.astype(F32) + grown).astype(BF16)
            if t + 1 == ITERS:
                layer_out[0, :, at] = out
            else:
                hout[t][n][...] = out

                @pl.when(s < 7)
                def _():
                    h_out(t, n).start()

    loads[0].wait()
    loads[1].wait()
    project(rows0[...], 0)
    kv[0][0][xc] = xs[0][y]
    spread(0)
    loads[2].wait()
    first_queries()

    @pl.when(s == 0)
    def _():
        for t in range(1, ITERS):
            for n in range(4):
                hid[t][n][...] = rows0[:, 512 * n:512 * n + 512]

    for t in range(ITERS):
        if t == 0:
            first_units()
        else:
            units(t)
        send_mixed(t)
        if t == 0:
            loads[3].wait()
        finish(t)
        if t + 1 < ITERS:
            @pl.when(top)
            def _():
                project(jnp.concatenate([hout[t][n][...] for n in range(4)], axis=1), t + 1)
                for s2 in range(7):
                    ks_out(t + 1, s2).start()
                kv[t + 1][0][xc] = xs[t + 1][3]

            @pl.when(s < 7)
            def _():
                ks_out(t + 1, 0).wait_recv()

            spread(t + 1)
            for d in range(7, 0, -1):
                @pl.when(d <= z)
                def _():
                    relay(t + 1, d)

            queries(t + 1)
            relay_own(t + 1)

    @pl.when(top)
    def _():
        project_last(layer_out[0])
        for s2 in range(7):
            ks_out(ITERS, s2).start()
        fin[c] = xf[7]

    @pl.when(s < 7)
    def _():
        ks_out(ITERS, 0).wait_recv()

    for d in range(1, 32):
        fin_out(d).start()

    def find(b, found):
        return jnp.where(block_slot[b] == c, b, found)

    block = lax.fori_loop(0, 32, find, jnp.int32(0))
    for d in range(1, 32):
        fin_in(d).wait_recv()
    rows = fin[block]
    decode[0, 0:HEAD, :] = rows[:, :HEAD]
    decode[0, HEAD:, :] = rows[:, HEAD:]

    for t in range(ITERS):
        spread_done(t)
        relay_done(t)
        for j in range(4):
            @pl.when(y != j)
            def _():
                q_out(t, j).wait_send()
                m_out(t, j).wait_send()
        if t + 1 < ITERS:
            @pl.when(s < 7)
            def _():
                for n in range(4):
                    h_out(t, n).wait_send()

        @pl.when(top)
        def _():
            for s2 in range(7):
                ks_out(t + 1, s2).wait_send()
    for d in range(1, 32):
        fin_out(d).wait_send()


def body(embeds, q_weight, out_weight, norm_gain, kv_weight, kv_gain, block_slot):
    vmem = pl.BlockSpec(memory_space=pltpu.VMEM)
    hbm = pl.BlockSpec(memory_space=pl.ANY)
    dma = pltpu.SemaphoreType.DMA
    return pl.pallas_call(
        kernel,
        out_shape=(
            jax.ShapeDtypeStruct((1, ROWS, WIDTH), BF16),
            jax.ShapeDtypeStruct((1, ROWS, HEAD), BF16),
        ),
        in_specs=[hbm, hbm, hbm, hbm, vmem, vmem, pl.BlockSpec(memory_space=pltpu.SMEM)],
        out_specs=(vmem, vmem),
        scratch_shapes=[
            pltpu.VMEM((WIDTH, 1024), BF16),
            pltpu.VMEM((1024, WIDTH), BF16),
            pltpu.VMEM((WIDTH, 512), BF16),
            (pltpu.VMEM((ROWS, WIDTH), BF16),) + (ITERS - 1) * (4 * (pltpu.VMEM((ROWS, 512), BF16),),),
            ITERS * (pltpu.VMEM((4, ROWS, 128), BF16),),
            pltpu.VMEM((8, HEAD, 128), BF16),
            ITERS * (8 * (pltpu.VMEM((4, ROWS, 128), BF16),),),
            ITERS * (pltpu.VMEM((4, 2, ROWS, 128), BF16),),
            ITERS * (pltpu.VMEM((4, 2, ROWS, 128), BF16),),
            ITERS * (pltpu.VMEM((4, ROWS, 256), BF16),),
            ITERS * (pltpu.VMEM((4, ROWS, 256), BF16),),
            (ITERS - 1) * (4 * (pltpu.VMEM((ROWS, 512), BF16),),),
            pltpu.VMEM((4096, 128), BF16),
            pltpu.VMEM((4096, 128), BF16),
            pltpu.VMEM((128, 4096), BF16),
            pltpu.VMEM((2, 8, 1024), F32),
            pltpu.VMEM((2, 72, 1024), F32),
            pltpu.VMEM((ROWS, 1024), F32),
            pltpu.VMEM((32, HEAD, 128), BF16),
            dma((4,)),
            dma((ITERS, 16)), dma((ITERS, 16)), dma((ITERS, 16)), dma((ITERS, 16)),
            dma((ITERS, 4)), dma((ITERS, 4)), dma((ITERS, 4)), dma((ITERS, 4)),
            dma((ITERS, 4)), dma((ITERS, 4)), dma((ITERS, 8)), dma((ITERS,)),
            dma((32,)), dma((32,)),
        ],
        compiler_params=pltpu.CompilerParams(
            collective_id=0, has_side_effects=True, vmem_limit_bytes=56 << 20
        ),
        cost_estimate=pl.CostEstimate(
            flops=20 * 10**9, bytes_accessed=12 * 2**20, transcendentals=10**7
        ),
    )(embeds, q_weight, out_weight, kv_weight, norm_gain, kv_gain, block_slot)


def solution(mesh):
    return jax.shard_map(
        body,
        mesh=mesh,
        in_specs=(
            P("ctx", None),
            P("section", None, None),
            P("section", None, None),
            P("section", None),
            P(),
            P(),
            P(),
        ),
        out_specs=(P("section", "ctx", None), P("ctx", None, "section")),
        check_vma=False,
    )
```

time: 167 us -> 138 us (0.83)
  Pallas kernels: 161 us -> 134 us
    pallas_call x1, Pallas kernels: 161 us -> 134 us  [body(): pl.pallas_call(kernel, out_shape=(jax.ShapeDtypeStruct((1, ROWS, WIDTH),...]
where the time goes in v2:
time: 138 us
  Pallas kernels  134 us (97%)
  local copies, waits for them, and re-layouts  3.33 us (2%)
    pallas_call x1, Pallas kernels, body(): pl.pallas_call(kernel, out_shape=(jax.ShapeDtypeStruct((1, ROWS, WIDTH),...  134 us

profile of v2, /device:TPU:1, one launch (start us, length us, event | category | flops | bytes accessed | tf_op | source)
XLA Modules:
  0.0 137.8 jit_solution(15067698922469757685)
XLA Ops:
  0.6 133.9 %shard_map.86 = (bf16[1,128,2048]{2,1,0:T(8,128)(2,1)}, bf16[1,128,64]{2,1,0:T(8,128)(2,1)}) custom-call(bf16[128,2048]{1,0:T(8,128)(2,1)} %embeds.1, bf16[1,2048,1024]{2,1,0:T(8,128)(2,1)} %q_weight.1, bf16[1,1024,2048]{2,1,0:T(8,128)(2,1)} %out_weight.1, bf16[2048,512]{1,0:T(8,128)(2,1)} %kv_weight.1, bf16[1,2048]{1,0:T(2,128)(2,1)} %norm_gain.1, ...), custom_call_target="tpu_custom_call" | custom-call | flops 20000000000 | bytes 12582912 | tf_op jit(solution)/shard_map/pallas_call | solution.py:442
  134.5 1.4 %copy.9 = bf16[1,128,64]{1,2,0:T(8,128)(2,1)} copy(bf16[1,128,64]{2,1,0:T(8,128)(2,1)} %get-tuple-element.3) | data formatting | bytes 32768 | tf_op jit(solution)/shard_map/pallas_call | solution.py:442
  135.9 1.9 %copy.11 = bf16[1,128,2048]{2,1,0:T(8,128)(2,1)} copy(bf16[1,128,2048]{2,1,0:T(8,128)(2,1)} %get-tuple-element.6) | data formatting | bytes 1048576

commit v3 on v2

--- a/solution.py
+++ b/solution.py
@@ -27,15 +27,16 @@
 def kernel(
     embeds, q_weight, out_weight, kv_weight, norm_gain, kv_gain, block_slot,
     layer_out, decode,
-    wq, wo, wkv, hid, xs, xf, kv, qst, qbuf, mst, mbuf, hout, ka, kb, vt, mx, acc, qacc, fin,
+    wq, wo, wkv, hid, xs, xf, kv, qst, qbuf, mst, mbuf, hout, ka, kb, vt, mx, acc, qacc, fin, pick, land,
     load_sem, kvd_s, kvd_r, sib_s, sib_r, q_s, q_r, m_s, m_r, h_s, h_r, ks_s, ks_r,
-    fin_s, fin_r,
+    fin_s, fin_r, pick_s, pick_r,
 ):
     s, c = lax.axis_index("section"), lax.axis_index("ctx")
     x_lo, y = s // 4, s % 4
     z, xh, core = c // 4, (c // 2) % 2, c % 2
     xc = c % 4
     top = s == 7
+    me = x_lo * 2 + y % 2
     sib = z * 4 + xh * 2 + (1 - core)
 
     rows0 = hid[0]
@@ -55,9 +56,12 @@
 
     for d in range(1, 8):
         greet((s + d) % 8, c)
-    for d in range(1, 32):
-        greet(s, (c + d) % 32)
-    pl.semaphore_wait(barrier, 7 + 31)
+    for d in range(1, 8):
+        for x2 in range(2):
+            greet(s, ((z + d) % 8) * 4 + x2 * 2 + core)
+    for d in range(1, 4):
+        greet(s, z * 4 + (xc + d) % 4)
+    pl.semaphore_wait(barrier, 7 + 14 + 3)
 
     def send(src, dst, ssem, rsem, section, ctx):
         return pltpu.make_async_remote_copy(
@@ -84,32 +88,39 @@
         return send(kv[t][d].at[b], kv[t][d].at[b], sib_s.at[t, d * 2 + x2],
                     sib_r.at[t, d * 2 + x2], s, sib)
 
+    def member(m):
+        return (m // 2) * 4 + (y // 2) * 2 + m % 2
+
     def q_out(t, j):
-        return send(qst[t].at[j], qbuf[t].at[y], q_s.at[t, j], q_r.at[t, y], x_lo * 4 + j, c)
+        return send(qst[t].at[j], qbuf[t].at[me], q_s.at[t, j], q_r.at[t, me], member(j), c)
 
     def q_in(t, j):
-        return send(qst[t].at[j], qbuf[t].at[j], q_s.at[t, j], q_r.at[t, j], x_lo * 4 + j, c)
+        return send(qst[t].at[j], qbuf[t].at[j], q_s.at[t, j], q_r.at[t, j], member(j), c)
 
     def m_out(t, i):
-        return send(mst[t].at[i], mbuf[t].at[y], m_s.at[t, i], m_r.at[t, y], x_lo * 4 + i, c)
+        return send(mst[t].at[i], mbuf[t].at[me], m_s.at[t, i], m_r.at[t, me], member(i), c)
 
     def m_in(t, j):
-        return send(mst[t].at[j], mbuf[t].at[j], m_s.at[t, j], m_r.at[t, j], x_lo * 4 + j, c)
+        return send(mst[t].at[j], mbuf[t].at[j], m_s.at[t, j], m_r.at[t, j], member(j), c)
 
     def h_out(t, n):
         return send(hout[t][n], hid[t + 1][n], h_s.at[t, n], h_r.at[t, n], (s + 1) % 8, c)
 
     def ks_out(t, s2):
         if t < ITERS:
-            return send(xs[t].at[s2 % 4], kv[t][0].at[xc], ks_s.at[t - 1, s2], ks_r.at[t - 1], s2, c)
-        return send(xf.at[s2], fin.at[c], ks_s.at[t - 1, s2], ks_r.at[t - 1], s2, c)
+            return send(xs[t].at[(s2 // 4) * 2 + s2 % 2], kv[t][0].at[xc], ks_s.at[t - 1, s2], ks_r.at[t - 1], s2, c)
+        return send(xf.at[s2], fin.at[z], ks_s.at[t - 1, s2], ks_r.at[t - 1], s2, c)
 
     def fin_out(d):
-        return send(fin.at[c], fin.at[c], fin_s.at[d], fin_r.at[d], s, (c + d) % 32)
+        return send(fin.at[z], fin.at[z], fin_s.at[d], fin_r.at[d], s, ((z + d) % 8) * 4 + xc)
 
     def fin_in(d):
-        b = (c + 32 - d) % 32
-        return send(fin.at[b], fin.at[b], fin_s.at[d], fin_r.at[d], s, b)
+        b = (z + 8 - d) % 8
+        return send(fin.at[b], fin.at[b], fin_s.at[d], fin_r.at[d], s, b * 4 + xc)
+
+    def pick_out(d):
+        other = (xc + d) % 4
+        return send(pick.at[d], land.at[d], pick_s.at[d], pick_r.at[d], s, z * 4 + other)
 
     lane = lax.broadcasted_iota(jnp.int32, (ROWS, 128), 1)
 
@@ -176,12 +187,12 @@
                     sib_out(t, d, x2).wait_send()
 
     def place_queries(t, j, rows):
-        @pl.when(y == j)
+        @pl.when(me == j)
         def _():
             for p in range(2):
                 qbuf[t][j, p] = rows[:, 128 * p:128 * p + 128]
 
-        @pl.when(y != j)
+        @pl.when(me != j)
         def _():
             for p in range(2):
                 qst[t][j, p] = rows[:, 128 * p:128 * p + 128]
@@ -253,7 +264,7 @@
 
     def wait_queries(t):
         for j in range(4):
-            @pl.when(y != j)
+            @pl.when(me != j)
             def _():
                 q_in(t, j).wait_recv()
 
@@ -291,18 +302,27 @@
 
     def units(t):
         start_state()
-        for d in range(7, 0, -1):
-            @pl.when(d <= z)
-            def _():
-                prepare(t, d)
+        for d in range(1, 8):
+            @pl.when(d == z)
+            def _():
+                relay(t, d)
 
         wait_queries(t)
 
-        def step(d, carry):
+        def step(i, carry):
+            d = z - i
+            for near in range(1, 8):
+                @pl.when(d == near)
+                def _():
+                    if near > 1:
+                        relay(t, near - 1)
+                    prepare(t, near)
+
             unit(t, d, False)
             return carry
 
-        lax.fori_loop(1, z + 1, step, 0)
+        lax.fori_loop(0, z, step, 0)
+        relay_own(t)
         prepare(t, 0)
         unit(t, 0, True)
 
@@ -313,21 +333,21 @@
                 halves = [acc[h, 0:HEAD, at] / acc[h, HEAD:HEAD + 1, at] for h in range(2)]
                 rows = jnp.concatenate(halves, axis=0).T.astype(BF16)
 
-                @pl.when(y == i)
+                @pl.when(me == i)
                 def _():
                     mbuf[t][i, :, 128 * p:128 * p + 128] = rows
 
-                @pl.when(y != i)
+                @pl.when(me != i)
                 def _():
                     mst[t][i, :, 128 * p:128 * p + 128] = rows
 
-            @pl.when(y != i)
+            @pl.when(me != i)
             def _():
                 m_out(t, i).start()
 
     def finish(t):
         for j in range(4):
-            @pl.when(y != j)
+            @pl.when(me != j)
             def _():
                 m_in(t, j).wait_recv()
         mixed = jnp.concatenate([mbuf[t][j] for j in range(4)], axis=1)
@@ -348,7 +368,7 @@
     loads[0].wait()
     loads[1].wait()
     project(rows0[...], 0)
-    kv[0][0][xc] = xs[0][y]
+    kv[0][0][xc] = xs[0][me]
     spread(0)
     loads[2].wait()
     first_queries()
@@ -376,40 +396,42 @@
                     ks_out(t + 1, s2).start()
                 kv[t + 1][0][xc] = xs[t + 1][3]
 
+            queries(t + 1)
+
             @pl.when(s < 7)
             def _():
                 ks_out(t + 1, 0).wait_recv()
 
             spread(t + 1)
-            for d in range(7, 0, -1):
-                @pl.when(d <= z)
-                def _():
-                    relay(t + 1, d)
-
-            queries(t + 1)
-            relay_own(t + 1)
 
     @pl.when(top)
     def _():
         project_last(layer_out[0])
         for s2 in range(7):
             ks_out(ITERS, s2).start()
-        fin[c] = xf[7]
+        fin[z] = xf[7]
 
     @pl.when(s < 7)
     def _():
         ks_out(ITERS, 0).wait_recv()
 
-    for d in range(1, 32):
+    for d in range(1, 8):
         fin_out(d).start()
 
     def find(b, found):
-        return jnp.where(block_slot[b] == c, b, found)
-
-    block = lax.fori_loop(0, 32, find, jnp.int32(0))
-    for d in range(1, 32):
+        slot = block_slot[b]
+        return tuple(jnp.where(slot == z * 4 + (xc + d) % 4, b, f) for d, f in enumerate(found))
+
+    found = lax.fori_loop(0, 32, find, (jnp.int32(0),) * 4)
+    for d in range(1, 8):
         fin_in(d).wait_recv()
-    rows = fin[block]
+    for d in range(1, 4):
+        pick[d] = fin[found[d] // 4]
+        pick_out(d).start()
+    rows = fin[found[0] // 4]
+    for d in range(1, 4):
+        pick_out(d).wait_recv()
+        rows = jnp.where(found[0] % 4 == (xc + 4 - d) % 4, land[d], rows)
     decode[0, 0:HEAD, :] = rows[:, :HEAD]
     decode[0, HEAD:, :] = rows[:, HEAD:]
 
@@ -417,7 +439,7 @@
         spread_done(t)
         relay_done(t)
         for j in range(4):
-            @pl.when(y != j)
+            @pl.when(me != j)
             def _():
                 q_out(t, j).wait_send()
                 m_out(t, j).wait_send()
@@ -431,8 +453,10 @@
         def _():
             for s2 in range(7):
                 ks_out(t + 1, s2).wait_send()
-    for d in range(1, 32):
+    for d in range(1, 8):
         fin_out(d).wait_send()
+    for d in range(1, 4):
+        pick_out(d).wait_send()
 
 
 def body(embeds, q_weight, out_weight, norm_gain, kv_weight, kv_gain, block_slot):
@@ -466,12 +490,14 @@
             pltpu.VMEM((2, 8, 1024), F32),
             pltpu.VMEM((2, 72, 1024), F32),
             pltpu.VMEM((ROWS, 1024), F32),
-            pltpu.VMEM((32, HEAD, 128), BF16),
+            pltpu.VMEM((8, HEAD, 128), BF16),
+            pltpu.VMEM((4, HEAD, 128), BF16),
+            pltpu.VMEM((4, HEAD, 128), BF16),
             dma((4,)),
             dma((ITERS, 16)), dma((ITERS, 16)), dma((ITERS, 16)), dma((ITERS, 16)),
             dma((ITERS, 4)), dma((ITERS, 4)), dma((ITERS, 4)), dma((ITERS, 4)),
             dma((ITERS, 4)), dma((ITERS, 4)), dma((ITERS, 8)), dma((ITERS,)),
-            dma((32,)), dma((32,)),
+            dma((8,)), dma((8,)), dma((4,)), dma((4,)),
         ],
         compiler_params=pltpu.CompilerParams(
             collective_id=0, has_side_effects=True, vmem_limit_bytes=56 << 20

time: 138 us -> 144 us (1.043)
  Pallas kernels: 134 us -> 140 us
    pallas_call x1, Pallas kernels: 134 us -> 140 us  [body(): pl.pallas_call(kernel, out_shape=(jax.ShapeDtypeStruct((1, ROWS, WIDTH),...]
where the time goes in v3:
time: 144 us
  Pallas kernels  140 us (97%)
  local copies, waits for them, and re-layouts  3.33 us (2%)
    pallas_call x1, Pallas kernels, body(): pl.pallas_call(kernel, out_shape=(jax.ShapeDtypeStruct((1, ROWS, WIDTH),...  140 us

profile of v3, /device:TPU:1, one launch (start us, length us, event | category | flops | bytes accessed | tf_op | source)
XLA Modules:
  0.0 143.6 jit_solution(2828632173779361933)
XLA Ops:
  0.6 139.6 %shard_map.86 = (bf16[1,128,2048]{2,1,0:T(8,128)(2,1)}, bf16[1,128,64]{2,1,0:T(8,128)(2,1)}) custom-call(bf16[128,2048]{1,0:T(8,128)(2,1)} %embeds.1, bf16[1,2048,1024]{2,1,0:T(8,128)(2,1)} %q_weight.1, bf16[1,1024,2048]{2,1,0:T(8,128)(2,1)} %out_weight.1, bf16[2048,512]{1,0:T(8,128)(2,1)} %kv_weight.1, bf16[1,2048]{1,0:T(2,128)(2,1)} %norm_gain.1, ...), custom_call_target="tpu_custom_call" | custom-call | flops 20000000000 | bytes 12582912 | tf_op jit(solution)/shard_map/pallas_call | solution.py:466
  140.2 1.4 %copy.9 = bf16[1,128,64]{1,2,0:T(8,128)(2,1)} copy(bf16[1,128,64]{2,1,0:T(8,128)(2,1)} %get-tuple-element.3) | data formatting | bytes 32768 | tf_op jit(solution)/shard_map/pallas_call | solution.py:466
  141.7 1.9 %copy.11 = bf16[1,128,2048]{2,1,0:T(8,128)(2,1)} copy(bf16[1,128,2048]{2,1,0:T(8,128)(2,1)} %get-tuple-element.6) | data formatting | bytes 1048576

commit v4 on v2

--- a/solution.py
+++ b/solution.py
@@ -27,7 +27,7 @@
 def kernel(
     embeds, q_weight, out_weight, kv_weight, norm_gain, kv_gain, block_slot,
     layer_out, decode,
-    wq, wo, wkv, hid, xs, xf, kv, qst, qbuf, mst, mbuf, hout, ka, kb, vt, mx, acc, qacc, fin,
+    wq, wo, wkv, hid, xs, xf, kv, qst, qbuf, mst, mbuf, hout, ka, kb, vt, mx, acc, sc, qacc, fin,
     load_sem, kvd_s, kvd_r, sib_s, sib_r, q_s, q_r, m_s, m_r, h_s, h_r, ks_s, ks_r,
     fin_s, fin_r,
 ):
@@ -36,6 +36,7 @@
     z, xh, core = c // 4, (c // 2) % 2, c % 2
     xc = c % 4
     top = s == 7
+    me = x_lo * 2 + y % 2
     sib = z * 4 + xh * 2 + (1 - core)
 
     rows0 = hid[0]
@@ -84,24 +85,27 @@
         return send(kv[t][d].at[b], kv[t][d].at[b], sib_s.at[t, d * 2 + x2],
                     sib_r.at[t, d * 2 + x2], s, sib)
 
+    def member(m):
+        return (m // 2) * 4 + (y // 2) * 2 + m % 2
+
     def q_out(t, j):
-        return send(qst[t].at[j], qbuf[t].at[y], q_s.at[t, j], q_r.at[t, y], x_lo * 4 + j, c)
+        return send(qst[t].at[j], qbuf[t].at[me], q_s.at[t, j], q_r.at[t, me], member(j), c)
 
     def q_in(t, j):
-        return send(qst[t].at[j], qbuf[t].at[j], q_s.at[t, j], q_r.at[t, j], x_lo * 4 + j, c)
+        return send(qst[t].at[j], qbuf[t].at[j], q_s.at[t, j], q_r.at[t, j], member(j), c)
 
     def m_out(t, i):
-        return send(mst[t].at[i], mbuf[t].at[y], m_s.at[t, i], m_r.at[t, y], x_lo * 4 + i, c)
+        return send(mst[t].at[i], mbuf[t].at[me], m_s.at[t, i], m_r.at[t, me], member(i), c)
 
     def m_in(t, j):
-        return send(mst[t].at[j], mbuf[t].at[j], m_s.at[t, j], m_r.at[t, j], x_lo * 4 + j, c)
+        return send(mst[t].at[j], mbuf[t].at[j], m_s.at[t, j], m_r.at[t, j], member(j), c)
 
     def h_out(t, n):
         return send(hout[t][n], hid[t + 1][n], h_s.at[t, n], h_r.at[t, n], (s + 1) % 8, c)
 
     def ks_out(t, s2):
         if t < ITERS:
-            return send(xs[t].at[s2 % 4], kv[t][0].at[xc], ks_s.at[t - 1, s2], ks_r.at[t - 1], s2, c)
+            return send(xs[t].at[(s2 // 4) * 2 + s2 % 2], kv[t][0].at[xc], ks_s.at[t - 1, s2], ks_r.at[t - 1], s2, c)
         return send(xf.at[s2], fin.at[c], ks_s.at[t - 1, s2], ks_r.at[t - 1], s2, c)
 
     def fin_out(d):
@@ -176,12 +180,12 @@
                     sib_out(t, d, x2).wait_send()
 
     def place_queries(t, j, rows):
-        @pl.when(y == j)
+        @pl.when(me == j)
         def _():
             for p in range(2):
                 qbuf[t][j, p] = rows[:, 128 * p:128 * p + 128]
 
-        @pl.when(y != j)
+        @pl.when(me != j)
         def _():
             for p in range(2):
                 qst[t][j, p] = rows[:, 128 * p:128 * p + 128]
@@ -228,32 +232,46 @@
         kb[at, :] = jnp.where(key_lane < HEAD, 0.0, r).astype(BF16)
         vt[:, at] = jnp.where(key_row < HEAD, r.T, 1.0).astype(BF16)
 
-    def unit(t, d, masked):
-        at = pl.ds(pl.multiple_of(d * 512, 512), 512)
-        qq = qbuf[t][...].reshape(1024, 128)
-        for h, keys in enumerate((ka, kb)):
-            scores = lax.dot_general(
-                keys[at, :], qq, (((1,), (1,)), ((), ())), preferred_element_type=F32
-            )
+    parts = [(h, slice(512 * half, 512 * half + 512)) for h in range(2) for half in range(2)]
+
+    def keys_at(d):
+        return pl.ds(pl.multiple_of(d * 512, 512), 512)
+
+    def score(t, d, part, slot):
+        h, cols = parts[part]
+        layers = slice(2 * (part % 2), 2 * (part % 2) + 2)
+        sc[slot] = lax.dot_general(
+            (ka, kb)[h][keys_at(d), :], qbuf[t][layers].reshape(512, 128),
+            (((1,), (1,)), ((), ())), preferred_element_type=F32,
+        )
+
+    def unit(t, d, after, masked):
+        for part, (h, cols) in enumerate(parts):
+            if part < 3:
+                score(t, d, part + 1, (part + 1) % 2)
+            elif after is not None:
+                score(t, after, 0, 0)
+            scores = sc[part % 2]
             if masked:
-                kpos = lax.broadcasted_iota(jnp.int32, (512, 1024), 0)
-                qpos = lax.broadcasted_iota(jnp.int32, (512, 1024), 1) % ROWS + xc * ROWS
+                kpos = lax.broadcasted_iota(jnp.int32, (512, 512), 0)
+                qpos = lax.broadcasted_iota(jnp.int32, (512, 512), 1) % ROWS + xc * ROWS
                 scores = jnp.where(kpos <= qpos, scores, NEG)
-            scores = scores.reshape(64, 8, 1024)
+            scores = scores.reshape(64, 8, 512)
             top8 = jnp.max(scores, axis=0)
             for k in (4, 2, 1):
                 top8 = jnp.maximum(top8, pltpu.roll(top8, k, 0))
-            old = mx[h]
+            old = mx[h, :, cols]
             new = jnp.maximum(old, top8)
             decay = jnp.exp2(old - new)
-            mx[h] = new
-            probs = jnp.exp2(scores - new[None]).astype(BF16).reshape(512, 1024)
-            grown = jnp.dot(vt[0:72, at], probs, preferred_element_type=F32)
-            acc[h] = (acc[h].reshape(9, 8, 1024) * decay[None]).reshape(72, 1024) + grown
+            mx[h, :, cols] = new
+            probs = jnp.exp2(scores - new[None]).astype(BF16).reshape(512, 512)
+            grown = jnp.dot(vt[0:72, keys_at(d)], probs, preferred_element_type=F32)
+            kept = (acc[h, :, cols].reshape(9, 8, 512) * decay[None]).reshape(72, 512)
+            acc[h, :, cols] = kept + grown
 
     def wait_queries(t):
         for j in range(4):
-            @pl.when(y != j)
+            @pl.when(me != j)
             def _():
                 q_in(t, j).wait_recv()
 
@@ -271,20 +289,30 @@
             relay(0, 1)
 
         wait_queries(0)
-        unit(0, 0, True)
+        score(0, 0, 0, 0)
+
+        @pl.when(z > 0)
+        def _():
+            prepare(0, 1)
+
+        unit(0, 0, jnp.minimum(z, 1), True)
+
+        @pl.when(z > 1)
+        def _():
+            relay(0, 2)
 
         def step(d, carry):
-            for near in range(1, 8):
-                @pl.when(d == near)
+            for near in range(1, 7):
+                @pl.when((d == near) & (near < z))
                 def _():
-                    if near < 7:
-                        @pl.when(near < z)
-                        def _():
-                            relay(0, near + 1)
-
-                    prepare(0, near)
-
-            unit(0, d, False)
+                    prepare(0, near + 1)
+
+            unit(0, d, jnp.minimum(d + 1, z), False)
+            for near in range(1, 6):
+                @pl.when((d == near) & (near + 1 < z))
+                def _():
+                    relay(0, near + 2)
+
             return carry
 
         lax.fori_loop(1, z + 1, step, 0)
@@ -297,14 +325,15 @@
                 prepare(t, d)
 
         wait_queries(t)
-
-        def step(d, carry):
-            unit(t, d, False)
+        prepare(t, 0)
+        score(t, z, 0, 0)
+
+        def step(i, carry):
+            unit(t, z - i, z - i - 1, False)
             return carry
 
-        lax.fori_loop(1, z + 1, step, 0)
-        prepare(t, 0)
-        unit(t, 0, True)
+        lax.fori_loop(0, z, step, 0)
+        unit(t, 0, None, True)
 
     def send_mixed(t):
         for i in range(4):
@@ -313,21 +342,21 @@
                 halves = [acc[h, 0:HEAD, at] / acc[h, HEAD:HEAD + 1, at] for h in range(2)]
                 rows = jnp.concatenate(halves, axis=0).T.astype(BF16)
 
-                @pl.when(y == i)
+                @pl.when(me == i)
                 def _():
                     mbuf[t][i, :, 128 * p:128 * p + 128] = rows
 
-                @pl.when(y != i)
+                @pl.when(me != i)
                 def _():
                     mst[t][i, :, 128 * p:128 * p + 128] = rows
 
-            @pl.when(y != i)
+            @pl.when(me != i)
             def _():
                 m_out(t, i).start()
 
     def finish(t):
         for j in range(4):
-            @pl.when(y != j)
+            @pl.when(me != j)
             def _():
                 m_in(t, j).wait_recv()
         mixed = jnp.concatenate([mbuf[t][j] for j in range(4)], axis=1)
@@ -348,7 +377,7 @@
     loads[0].wait()
     loads[1].wait()
     project(rows0[...], 0)
-    kv[0][0][xc] = xs[0][y]
+    kv[0][0][xc] = xs[0][me]
     spread(0)
     loads[2].wait()
     first_queries()
@@ -417,7 +446,7 @@
         spread_done(t)
         relay_done(t)
         for j in range(4):
-            @pl.when(y != j)
+            @pl.when(me != j)
             def _():
                 q_out(t, j).wait_send()
                 m_out(t, j).wait_send()
@@ -465,6 +494,7 @@
             pltpu.VMEM((128, 4096), BF16),
             pltpu.VMEM((2, 8, 1024), F32),
             pltpu.VMEM((2, 72, 1024), F32),
+            pltpu.VMEM((2, 512, 512), F32),
             pltpu.VMEM((ROWS, 1024), F32),
             pltpu.VMEM((32, HEAD, 128), BF16),
             dma((4,)),

time: 138 us -> 136 us (0.986)
  Pallas kernels: 134 us -> 131 us
    pallas_call x1, Pallas kernels: 134 us -> 131 us  [body(): pl.pallas_call(kernel, out_shape=(jax.ShapeDtypeStruct((1, ROWS, WIDTH),...]
where the time goes in v4:
time: 136 us; the launch traced here: 135 us
  Pallas kernels  131 us (96%)
  local copies, waits for them, and re-layouts  3.33 us (2%)
    pallas_call x1, Pallas kernels, body(): pl.pallas_call(kernel, out_shape=(jax.ShapeDtypeStruct((1, ROWS, WIDTH),...  131 us

profile of v4, /device:TPU:1, one launch (start us, length us, event | category | flops | bytes accessed | tf_op | source)
XLA Modules:
  0.0 135.1 jit_solution(6430324284322124444)
XLA Ops:
  0.6 131.1 %shard_map.86 = (bf16[1,128,2048]{2,1,0:T(8,128)(2,1)}, bf16[1,128,64]{2,1,0:T(8,128)(2,1)}) custom-call(bf16[128,2048]{1,0:T(8,128)(2,1)} %embeds.1, bf16[1,2048,1024]{2,1,0:T(8,128)(2,1)} %q_weight.1, bf16[1,1024,2048]{2,1,0:T(8,128)(2,1)} %out_weight.1, bf16[2048,512]{1,0:T(8,128)(2,1)} %kv_weight.1, bf16[1,2048]{1,0:T(2,128)(2,1)} %norm_gain.1, ...), custom_call_target="tpu_custom_call" | custom-call | flops 20000000000 | bytes 12582912 | tf_op jit(solution)/shard_map/pallas_call | solution.py:471
  131.8 1.4 %copy.9 = bf16[1,128,64]{1,2,0:T(8,128)(2,1)} copy(bf16[1,128,64]{2,1,0:T(8,128)(2,1)} %get-tuple-element.3) | data formatting | bytes 32768 | tf_op jit(solution)/shard_map/pallas_call | solution.py:471
  133.2 1.9 %copy.11 = bf16[1,128,2048]{2,1,0:T(8,128)(2,1)} copy(bf16[1,128,2048]{2,1,0:T(8,128)(2,1)} %get-tuple-element.6) | data formatting | bytes 1048576

commit v5 on v4

--- a/solution.py
+++ b/solution.py
@@ -28,7 +28,7 @@
     embeds, q_weight, out_weight, kv_weight, norm_gain, kv_gain, block_slot,
     layer_out, decode,
     wq, wo, wkv, hid, xs, xf, kv, qst, qbuf, mst, mbuf, hout, ka, kb, vt, mx, acc, sc, qacc, fin,
-    load_sem, kvd_s, kvd_r, sib_s, sib_r, q_s, q_r, m_s, m_r, h_s, h_r, ks_s, ks_r,
+    load_sem, kvd_s, kvd_r, x_s, x_r, sib_s, sib_r, q_s, q_r, m_s, m_r, h_s, h_r, ks_s, ks_r,
     fin_s, fin_r,
 ):
     s, c = lax.axis_index("section"), lax.axis_index("ctx")
@@ -38,6 +38,7 @@
     top = s == 7
     me = x_lo * 2 + y % 2
     sib = z * 4 + xh * 2 + (1 - core)
+    across = z * 4 + (1 - xh) * 2 + core
 
     rows0 = hid[0]
     loads = [
@@ -66,14 +67,18 @@
             device_id=(section, ctx), device_id_type=MESH,
         )
 
-    def kv_out(t, d, x2):
-        return send(kv[t][0].at[xc], kv[t][d].at[xc], kvd_s.at[t, d * 2 + x2],
-                    kvd_r.at[t, d * 2 + xh], s, (z + d) * 4 + x2 * 2 + core)
-
-    def kv_in(t, d, x2):
-        b = x2 * 2 + core
-        return send(kv[t][d].at[b], kv[t][d].at[b], kvd_s.at[t, d * 2 + x2],
-                    kvd_r.at[t, d * 2 + x2], s, sib)
+    def kv_out(t, d):
+        return send(kv[t][0].at[xc], kv[t][d].at[xc], kvd_s.at[t, d], kvd_r.at[t, d], s, (z + d) * 4 + xc)
+
+    def kv_in(t, d):
+        return send(kv[t][d].at[xc], kv[t][d].at[xc], kvd_s.at[t, d], kvd_r.at[t, d], s, sib)
+
+    def x_out(t, d):
+        return send(kv[t][d].at[xc], kv[t][d].at[xc], x_s.at[t, d], x_r.at[t, d], s, across)
+
+    def x_in(t, d):
+        b = (1 - xh) * 2 + core
+        return send(kv[t][d].at[b], kv[t][d].at[b], x_s.at[t, d], x_r.at[t, d], s, across)
 
     def sib_out(t, d, x2):
         b = x2 * 2 + core
@@ -146,38 +151,33 @@
 
     def spread(t):
         sib_out(t, 0, xh).start()
-        kv_out(t, 0, 1 - xh).start()
+        x_out(t, 0).start()
         for d in range(1, 8):
             @pl.when(z + d < 8)
             def _():
-                for x2 in range(2):
-                    kv_out(t, d, x2).start()
+                kv_out(t, d).start()
+
+    def relay(t, d):
+        kv_in(t, d).wait_recv()
+        sib_out(t, d, xh).start()
+        x_out(t, d).start()
+
+    def relay_across(t, d):
+        x_in(t, d).wait_recv()
+        sib_out(t, d, 1 - xh).start()
 
     def spread_done(t):
-        sib_out(t, 0, xh).wait_send()
-        kv_out(t, 0, 1 - xh).wait_send()
-        for d in range(1, 8):
-            @pl.when(z + d < 8)
-            def _():
-                for x2 in range(2):
-                    kv_out(t, d, x2).wait_send()
-
-    def relay(t, d):
-        for x2 in range(2):
-            kv_in(t, d, x2).wait_recv()
-            sib_out(t, d, x2).start()
-
-    def relay_own(t):
-        kv_in(t, 0, 1 - xh).wait_recv()
-        sib_out(t, 0, 1 - xh).start()
-
-    def relay_done(t):
-        sib_out(t, 0, 1 - xh).wait_send()
-        for d in range(1, 8):
+        for d in range(8):
             @pl.when(d <= z)
             def _():
+                x_out(t, d).wait_send()
                 for x2 in range(2):
                     sib_out(t, d, x2).wait_send()
+
+            if d > 0:
+                @pl.when(z + d < 8)
+                def _():
+                    kv_out(t, d).wait_send()
 
     def place_queries(t, j, rows):
         @pl.when(me == j)
@@ -281,38 +281,39 @@
 
     def first_units():
         start_state()
-        relay_own(0)
-        prepare(0, 0)
+        relay_across(0, 0)
 
         @pl.when(z > 0)
         def _():
             relay(0, 1)
 
+        prepare(0, 0)
         wait_queries(0)
         score(0, 0, 0, 0)
-
-        @pl.when(z > 0)
-        def _():
-            prepare(0, 1)
-
-        unit(0, 0, jnp.minimum(z, 1), True)
-
-        @pl.when(z > 1)
-        def _():
-            relay(0, 2)
+        unit(0, 0, None, True)
+
+        def pass_on(d):
+            for near in range(0, 7):
+                @pl.when((d == near) & (near < z))
+                def _():
+                    if near < 6:
+                        @pl.when(near + 1 < z)
+                        def _():
+                            relay(0, near + 2)
+
+                    relay_across(0, near + 1)
+
+        pass_on(0)
 
         def step(d, carry):
-            for near in range(1, 7):
-                @pl.when((d == near) & (near < z))
-                def _():
-                    prepare(0, near + 1)
-
-            unit(0, d, jnp.minimum(d + 1, z), False)
-            for near in range(1, 6):
-                @pl.when((d == near) & (near + 1 < z))
-                def _():
-                    relay(0, near + 2)
-
+            for near in range(1, 8):
+                @pl.when(d == near)
+                def _():
+                    prepare(0, near)
+
+            score(0, d, 0, 0)
+            unit(0, d, None, False)
+            pass_on(d)
             return carry
 
         lax.fori_loop(1, z + 1, step, 0)
@@ -416,7 +417,10 @@
                     relay(t + 1, d)
 
             queries(t + 1)
-            relay_own(t + 1)
+            for d in range(7, -1, -1):
+                @pl.when(d <= z)
+                def _():
+                    relay_across(t + 1, d)
 
     @pl.when(top)
     def _():
@@ -444,7 +448,6 @@
 
     for t in range(ITERS):
         spread_done(t)
-        relay_done(t)
         for j in range(4):
             @pl.when(me != j)
             def _():
@@ -498,7 +501,7 @@
             pltpu.VMEM((ROWS, 1024), F32),
             pltpu.VMEM((32, HEAD, 128), BF16),
             dma((4,)),
-            dma((ITERS, 16)), dma((ITERS, 16)), dma((ITERS, 16)), dma((ITERS, 16)),
+            dma((ITERS, 8)), dma((ITERS, 8)), dma((ITERS, 8)), dma((ITERS, 8)), dma((ITERS, 16)), dma((ITERS, 16)),
             dma((ITERS, 4)), dma((ITERS, 4)), dma((ITERS, 4)), dma((ITERS, 4)),
             dma((ITERS, 4)), dma((ITERS, 4)), dma((ITERS, 8)), dma((ITERS,)),
             dma((32,)), dma((32,)),

time: 136 us -> 142 us (1.044)
  Pallas kernels: 131 us -> 138 us
    pallas_call x1, Pallas kernels: 131 us -> 138 us  [body(): pl.pallas_call(kernel, out_shape=(jax.ShapeDtypeStruct((1, ROWS, WIDTH),...]
where the time goes in v5:
time: 142 us
  Pallas kernels  138 us (97%)
  local copies, waits for them, and re-layouts  3.33 us (2%)
    pallas_call x1, Pallas kernels, body(): pl.pallas_call(kernel, out_shape=(jax.ShapeDtypeStruct((1, ROWS, WIDTH),...  138 us

profile of v5, /device:TPU:1, one launch (start us, length us, event | category | flops | bytes accessed | tf_op | source)
XLA Modules:
  0.0 141.7 jit_solution(463461756477876428)
XLA Ops:
  0.6 137.7 %shard_map.86 = (bf16[1,128,2048]{2,1,0:T(8,128)(2,1)}, bf16[1,128,64]{2,1,0:T(8,128)(2,1)}) custom-call(bf16[128,2048]{1,0:T(8,128)(2,1)} %embeds.1, bf16[1,2048,1024]{2,1,0:T(8,128)(2,1)} %q_weight.1, bf16[1,1024,2048]{2,1,0:T(8,128)(2,1)} %out_weight.1, bf16[2048,512]{1,0:T(8,128)(2,1)} %kv_weight.1, bf16[1,2048]{1,0:T(2,128)(2,1)} %norm_gain.1, ...), custom_call_target="tpu_custom_call" | custom-call | flops 20000000000 | bytes 12582912 | tf_op jit(solution)/shard_map/pallas_call | solution.py:474
  138.3 1.4 %copy.9 = bf16[1,128,64]{1,2,0:T(8,128)(2,1)} copy(bf16[1,128,64]{2,1,0:T(8,128)(2,1)} %get-tuple-element.3) | data formatting | bytes 32768 | tf_op jit(solution)/shard_map/pallas_call | solution.py:474
  139.8 1.9 %copy.11 = bf16[1,128,2048]{2,1,0:T(8,128)(2,1)} copy(bf16[1,128,2048]{2,1,0:T(8,128)(2,1)} %get-tuple-element.6) | data formatting | bytes 1048576

commit v6 on v4

--- a/solution.py
+++ b/solution.py
@@ -290,29 +290,21 @@
 
         wait_queries(0)
         score(0, 0, 0, 0)
-
-        @pl.when(z > 0)
-        def _():
-            prepare(0, 1)
-
-        unit(0, 0, jnp.minimum(z, 1), True)
-
-        @pl.when(z > 1)
-        def _():
-            relay(0, 2)
+        unit(0, 0, None, True)
 
         def step(d, carry):
-            for near in range(1, 7):
-                @pl.when((d == near) & (near < z))
+            for near in range(1, 8):
+                @pl.when(d == near)
                 def _():
-                    prepare(0, near + 1)
-
-            unit(0, d, jnp.minimum(d + 1, z), False)
-            for near in range(1, 6):
-                @pl.when((d == near) & (near + 1 < z))
-                def _():
-                    relay(0, near + 2)
-
+                    if near < 7:
+                        @pl.when(near < z)
+                        def _():
+                            relay(0, near + 1)
+
+                    prepare(0, near)
+
+            score(0, d, 0, 0)
+            unit(0, d, None, False)
             return carry
 
         lax.fori_loop(1, z + 1, step, 0)

time: 136 us -> 133 us (0.978)
  Pallas kernels: 131 us -> 128 us
    pallas_call x1, Pallas kernels: 131 us -> 128 us  [body(): pl.pallas_call(kernel, out_shape=(jax.ShapeDtypeStruct((1, ROWS, WIDTH),...]
where the time goes in v6:
time: 133 us; the launch traced here: 132 us
  Pallas kernels  128 us (96%)
  local copies, waits for them, and re-layouts  3.33 us (3%)
    pallas_call x1, Pallas kernels, body(): pl.pallas_call(kernel, out_shape=(jax.ShapeDtypeStruct((1, ROWS, WIDTH),...  128 us

profile of v6, /device:TPU:1, one launch (start us, length us, event | category | flops | bytes accessed | tf_op | source)
XLA Modules:
  0.0 131.9 jit_solution(3370987860588651321)
XLA Ops:
  0.6 128.0 %shard_map.86 = (bf16[1,128,2048]{2,1,0:T(8,128)(2,1)}, bf16[1,128,64]{2,1,0:T(8,128)(2,1)}) custom-call(bf16[128,2048]{1,0:T(8,128)(2,1)} %embeds.1, bf16[1,2048,1024]{2,1,0:T(8,128)(2,1)} %q_weight.1, bf16[1,1024,2048]{2,1,0:T(8,128)(2,1)} %out_weight.1, bf16[2048,512]{1,0:T(8,128)(2,1)} %kv_weight.1, bf16[1,2048]{1,0:T(2,128)(2,1)} %norm_gain.1, ...), custom_call_target="tpu_custom_call" | custom-call | flops 20000000000 | bytes 12582912 | tf_op jit(solution)/shard_map/pallas_call | solution.py:463
  128.6 1.4 %copy.9 = bf16[1,128,64]{1,2,0:T(8,128)(2,1)} copy(bf16[1,128,64]{2,1,0:T(8,128)(2,1)} %get-tuple-element.3) | data formatting | bytes 32768 | tf_op jit(solution)/shard_map/pallas_call | solution.py:463
  130.0 1.9 %copy.11 = bf16[1,128,2048]{2,1,0:T(8,128)(2,1)} copy(bf16[1,128,2048]{2,1,0:T(8,128)(2,1)} %get-tuple-element.6) | data formatting | bytes 1048576
